TPU v7x, 128 devices: a whole 4x4x4 slice. The times are simulated.
128 devices in a mesh: dp: 8 (over z, y_hi), mp: 16 (over y_lo, x, core).
Axes of the slice: x: 4, y: 4 (y_hi: 2, y_lo: 2; y = y_hi * 2 + y_lo), z: 4, core: 2. Of those that a mesh axis runs over, the one named last changes fastest.
Arguments:
- grads: bfloat16 [8, 128, 8192, 128], P('dp', None, 'mp')
- momentum: bfloat16 [8, 16, 2, 8192, 128], P('dp', 'mp'), may hold values from -6 to 6
- owner_table: int32 [8, 16, 2], P('dp'), may hold values from 0 to 16, as said below
Outputs:
- update: bfloat16 [128, 8192, 128], P('dp', 'mp')
- new_momentum: bfloat16 [8, 16, 2, 8192, 128], P('dp', 'mp')
Inputs may be any that keep to these rules, and one draw needn't show every extreme that they name: For each index d of dp, the 16 x 2 entries owner_table[d] name each matrix 0 to 15 of the group exactly once, and every other slot holds 16, meaning empty. In every group some owner has all 2 slots filled.
All inputs are finite; a program needn't handle non-finite values.
Results may differ from a plain program's by a relative error of at most 0.025.
Values may be sent and summed in bfloat16 or wider, within the bound.
No kernel may reach another device: no remote copies, remote signals or barrier semaphores. Data moves between devices by JAX's collectives and lax.ppermute only.
A program may use at most 128 MiB of HBM per device.

v0:
```python
import math

import jax
import jax.numpy as jnp
from jax import lax
from jax.sharding import PartitionSpec as P

ROWS = 8192
HEAD = 128
ITERS = 2


momentum_rate = 0.95
coef_first = 3.4445
coef_second = -4.775
coef_third = 2.0315
norm_eps = 1e-07


def locate(owners, group_count):
    flat_owners = owners.T.reshape(-1)
    index = jnp.arange(flat_owners.shape[0], dtype=jnp.int32)
    wanted = jnp.arange(group_count, dtype=jnp.int32)
    hits = flat_owners[None, :] == wanted[:, None]
    return jnp.sum(jnp.where(hits, index[None, :], 0), axis=1)


def iterate_all(iterate, reduce_gram):
    for iteration in range(ITERS):
        gram = reduce_gram(
            jnp.einsum("mrh,mrk->mhk", iterate, iterate, preferred_element_type=jnp.float32)
        )
        gram_half = gram.astype(jnp.bfloat16)
        square = jnp.einsum(
            "mij,mjk->mik", gram_half, gram_half, preferred_element_type=jnp.float32
        )
        poly = (coef_second * gram_half.astype(jnp.float32) + coef_third * square).astype(
            jnp.bfloat16
        )
        turned = jnp.einsum("mrh,mhk->mrk", iterate, poly, preferred_element_type=jnp.float32)
        iterate = (coef_first * iterate.astype(jnp.float32) + turned).astype(jnp.bfloat16)
    return (math.sqrt(ROWS) * iterate.astype(jnp.float32)).astype(jnp.bfloat16)


def keep_gram(gram):
    return gram


def on_device(grads, momentum, owner_table):
    owners = owner_table[0]
    mp_size = lax.axis_size("mp")
    slot_count = owners.shape[1]
    summed = lax.psum_scatter(
        grads[0].astype(jnp.float32).astype(jnp.bfloat16), "dp", scatter_dimension=0, tiled=True
    ).astype(jnp.float32)
    group_count = summed.shape[0]
    piece_rows = summed.shape[1]
    placed = locate(owners, group_count)
    stored = momentum[0, 0]
    outgoing = jnp.take(summed, owners.T, axis=0, mode="fill", fill_value=0.0)
    whole = (
        lax.all_to_all(outgoing.astype(jnp.bfloat16), "mp", split_axis=1, concat_axis=1, tiled=True)
        .astype(outgoing.dtype)
        .reshape(slot_count, -1, HEAD)
    )
    renewed = (momentum_rate * stored.astype(jnp.float32) + whole).astype(jnp.bfloat16)
    mixed = whole + momentum_rate * renewed.astype(jnp.float32)
    length = jnp.sqrt(jnp.sum(mixed * mixed, axis=(1, 2)))
    start = (mixed / (length + norm_eps)[:, None, None]).astype(jnp.bfloat16)
    finished = iterate_all(start, keep_gram)
    returned = lax.all_to_all(
        finished.reshape(slot_count, mp_size, piece_rows, HEAD),
        "mp",
        split_axis=1,
        concat_axis=1,
        tiled=True,
    )
    update = jnp.take(returned.reshape(slot_count * mp_size, piece_rows, HEAD), placed, axis=0)
    return (update, renewed[None, None])


def solution(mesh):
    in_specs = (P("dp", None, "mp", None), P("dp", "mp", None, None, None), P("dp", None, None))
    out_specs = (P("dp", "mp", None), P("dp", "mp", None, None, None))
    return jax.shard_map(
        on_device, mesh=mesh, in_specs=in_specs, out_specs=out_specs, check_vma=False
    )
```

profile of v0, /device:TPU:1, one launch (start us, length us, event | category | flops | bytes accessed | tf_op | source)
XLA Modules:
  0.0 399.8 jit_solution(4612744745707724515)
XLA Ops:
  7.2 0.0 reduce-scatter.2.cloned.1.call-start
  7.2 0.0 copy-start.3
  7.2 0.7 reduce-scatter.2.cloned.1.call-update
  7.9 0.0 copy-done.3
  7.9 0.1 reshape.57
  8.0 197.3 %reduce-scatter.2.cloned.1.call-done = bf16[16,512,128]{2,1,0:T(8,128)(2,1)} async-done(((bf16[128,512,128]{2,1,0:T(8,128)(2,1)}), bf16[16,512,128]{2,1,0:T(8,128)(2,1)}) %reduce-scatter.2.cloned.1.call-update) | async-done | bytes 2097168 | tf_op jit(solution)/shard_map/reduce_scatter | solution.py:53
  205.4 4.7 %gather_fusion = bf16[32,512,128]{2,1,0:T(8,128)(2,1)} fusion(bf16[16,512,128]{2,1,0:T(8,128)(2,1)} %reduce-scatter.2.cloned.1.call-done, s32[1024]{0:T(1024)S(1)} %pad_clamp_fusion.1), kind=kCustom, calls=%fused_computation | custom fusion | bytes 8388736 | tf_op jit(solution)/shard_map/jit(_take)/gather | solution.py:60
  210.1 3.4 select_convert_fusion
  213.5 0.4 copy.25
  213.9 57.3 %all_to_all.10 = bf16[2,16,512,128]{3,2,0,1:T(8,128)(2,1)S(1)} all-to-all(bf16[2,16,512,128]{3,2,0,1:T(8,128)(2,1)S(1)} %copy.25), channel_id=1, replica_groups=mesh['dp'=8,'mp'=16] {'mp'}, dimensions={1} | all-to-all | bytes 8388608 | tf_op jit(solution)/shard_map/all_to_all | solution.py:62
  271.2 4.2 %copy.26 = f32[2,16,512,128]{3,2,1,0:T(8,128)} copy(bf16[2,16,512,128]{3,2,0,1:T(8,128)(2,1)S(1)} %all_to_all.10) | data formatting | bytes 12582912 | tf_op jit(solution)/shard_map/convert_element_type | solution.py:63
  275.4 10.6 %add_convert_fusion = (bf16[1,1,2,8192,128]{4,3,2,1,0:T(8,128)(2,1)}, f32[1,1,2,8192,128]{4,3,2,1,0:T(8,128)}) fusion(f32[1,1,2,8192,128]{4,3,2,1,0:T(8,128)} %bitcast.41, bf16[1,1,2,8192,128]{4,3,2,1,0:T(8,128)(2,1)} %param.4), kind=kLoop, calls=%fused_computation.16 | loop fusion | flops 8388608 | bytes 25165824 | tf_op jit(solution)/shard_map/convert_element_type | solution.py:66
  286.0 0.0 copy-start.1
  286.0 0.0 copy-start.2
  286.0 4.8 %multiply_reduce_fusion = f32[2]{0:T(128)S(1)} fusion(f32[2,16,512,128]{3,2,1,0:T(8,128)} %bitcast.42, bf16[2,16,512,128]{3,2,0,1:T(8,128)(2,1)S(1)} %all_to_all.10), kind=kLoop, calls=%fused_computation.17 | loop fusion | flops 16777214 | bytes 12582920 | tf_op jit(solution)/shard_map/reduce_sum | solution.py:68
  290.8 1.0 copy-done.1
  291.8 1.2 copy-done.2
  293.0 2.5 fusion.7
  295.5 0.0 copy-start
  295.6 2.0 copy-done
  297.5 1.4 convolution_convert_fusion.1
  298.9 6.9 %fusion = bf16[2,8192,128]{2,1,0:T(8,128)(2,1)} fusion(bf16[2,8192,128]{2,1,0:T(8,128)(2,1)} %copy-done, bf16[2,128,128]{2,1,0:T(8,128)(2,1)S(1)} %convolution_convert_fusion.1), kind=kOutput, calls=%fused_computation.4 | convolution fusion | flops 553811968 | bytes 8454144 | tf_op jit(solution)/shard_map/mrh,mhk->mrk/dot_general | solution.py:40
  305.8 4.8 %convolution_convert_fusion = bf16[2,128,128]{2,1,0:T(8,128)(2,1)S(1)} fusion(bf16[2,8192,128]{2,1,0:T(8,128)(2,1)} %fusion), kind=kOutput, calls=%fused_computation.27 | convolution fusion | flops 536903680 | bytes 4259840 | tf_op jit(solution)/shard_map/mrh,mrk->mhk/dot_general | solution.py:31
  310.6 7.2 %fusion.4 = bf16[2,8192,128]{2,1,0:T(8,128)(2,1)} fusion(bf16[2,8192,128]{2,1,0:T(8,128)(2,1)} %fusion, bf16[2,128,128]{2,1,0:T(8,128)(2,1)S(1)} %convolution_convert_fusion), kind=kOutput, calls=%fused_computation.8 | convolution fusion | flops 560103424 | bytes 8454144 | tf_op jit(solution)/shard_map/mrh,mhk->mrk/dot_general | solution.py:40
  317.9 4.6 %copy.30 = bf16[2,16,512,128]{3,2,0,1:T(8,128)(2,1)} copy(bf16[2,16,512,128]{3,2,1,0:T(8,128)(2,1)} %bitcast.46) | data formatting | bytes 8388608 | tf_op jit(solution)/shard_map/reshape | solution.py:72
  322.5 5.3 %all-to-all-start.1 = ((bf16[2,16,512,128]{3,2,0,1:T(8,128)(2,1)}), bf16[2,16,512,128]{3,2,0,1:T(8,128)(2,1)}, u32[]{:S(2)}, u32[]{:S(2)}) async-start(bf16[2,16,512,128]{3,2,0,1:T(8,128)(2,1)} %copy.30), calls=%async_computation.2 | async-start | bytes 8388608 | tf_op jit(solution)/shard_map/all_to_all | solution.py:71
  327.8 0.1 eq.15
  327.9 0.1 select_reduce_fusion
  328.0 55.6 %all-to-all-done.1 = bf16[2,16,512,128]{3,2,0,1:T(8,128)(2,1)} async-done(((bf16[2,16,512,128]{3,2,0,1:T(8,128)(2,1)}), bf16[2,16,512,128]{3,2,0,1:T(8,128)(2,1)}, u32[]{:S(2)}, u32[]{:S(2)}) %all-to-all-start.1) | async-done | bytes 4194336 | tf_op jit(solution)/shard_map/all_to_all | solution.py:71
  383.6 4.6 %copy.31 = bf16[2,16,512,128]{3,2,1,0:T(8,128)(2,1)} copy(bf16[2,16,512,128]{3,2,0,1:T(8,128)(2,1)} %all-to-all-done.1) | data formatting | bytes 8388608 | tf_op jit(solution)/shard_map/all_to_all | solution.py:71
  388.2 3.1 gather_fusion.1
  391.4 1.6 broadcast_select_fusion
  (7 shorter events, 0.1 us)
Async XLA Ops:
  7.2 198.2 %reduce-scatter.2.cloned.1.call-start = ((), (), s32[]{:S(2)}) async-start(), calls=%async_computation.3 | async-start | bytes 18874368 | tf_op jit(solution)/shard_map/reduce_scatter | solution.py:53
  7.2 0.7 copy-start.3
  286.0 5.8 %copy-start.1 = (f32[2,16,512,128]{3,2,1,0:T(8,128)S(1)}, f32[2,16,512,128]{3,2,1,0:T(8,128)}, u32[]{:S(2)}) copy-start(f32[2,16,512,128]{3,2,1,0:T(8,128)} %copy.26) | copy-start | bytes 25165828
  286.0 7.0 %copy-start.2 = (bf16[1,1,2,8192,128]{4,3,2,1,0:T(8,128)(2,1)S(1)}, bf16[1,1,2,8192,128]{4,3,2,1,0:T(8,128)(2,1)}, u32[]{:S(2)}) copy-start(bf16[1,1,2,8192,128]{4,3,2,1,0:T(8,128)(2,1)} %param.4) | copy-start | bytes 12582916
  295.5 2.0 copy-start
  322.5 61.1 %all-to-all-start.1 = ((bf16[2,16,512,128]{3,2,0,1:T(8,128)(2,1)}), bf16[2,16,512,128]{3,2,0,1:T(8,128)(2,1)}, u32[]{:S(2)}, u32[]{:S(2)}) async-start(bf16[2,16,512,128]{3,2,0,1:T(8,128)(2,1)} %copy.30), calls=%async_computation.2 | async-start | bytes 8388608 | tf_op jit(solution)/shard_map/all_to_all | solution.py:71
Sparse Core Ops, SparseCore 0:
  12.0 193.3 reduce-scatter.1
where the time goes:
time: 400 us
  waiting for transfers between devices  254 us (64%)
  blocking collectives  57.3 us (14%)
  local copies, waits for them, and re-layouts  26 us (6%)
  other arithmetic  23.1 us (6%)
  matrix products  20.4 us (5%)
  between operations  14.1 us (4%)
  starting transfers between devices  5.37 us (1%)
    reduce_scatter x1, waiting for transfers between devices, on_device(): lax.psum_scatter(grads[0].astype(jnp.float32).astype(jnp.bfloat16), 'dp',...  197 us
    all_to_all x1, blocking collectives, on_device(): lax.all_to_all(outgoing.astype(jnp.bfloat16), 'mp', split_axis=1, concat_...  57.3 us
    all_to_all x1, waiting for transfers between devices, on_device(): lax.all_to_all(finished.reshape(slot_count, mp_size, piece_rows, HEAD), '...  55.6 us
    dot_general x2, matrix products, iterate_all(): jnp.einsum('mrh,mhk->mrk', iterate, poly, preferred_element_type=jnp.floa...  14.1 us
    convert_element_type x1, other arithmetic, on_device(): (momentum_rate * stored.astype(jnp.float32) + whole).astype(jnp.bfloat16)  10.6 us
  transfers between devices with their start and end apart: 2, of which 2 were waited for; matrix products, arithmetic and copies ran while one was open for 0% of the time, Pallas kernels for 0%

commit v1 on v0

v1 whole, which is shorter than its diff:
```python
import math

import jax
import jax.numpy as jnp
from jax import lax
from jax.experimental import pallas as pl
from jax.experimental.pallas import tpu as pltpu
from jax.sharding import PartitionSpec as P

ROWS = 8192
HEAD = 128
ITERS = 2

momentum_rate = 0.95
coef_first = 3.4445
coef_second = -4.775
coef_third = 2.0315
norm_eps = 1e-07

Z_SIZE = 4
Y_SIZE = 2
CHUNKS = ((0, 256, False), (256, 128, False), (384, 128, True))
VMEM = 48 * 1024 * 1024


def params():
    return pltpu.CompilerParams(vmem_limit_bytes=VMEM)


def z_groups():
    return [[z * Y_SIZE + y for z in range(Z_SIZE)] for y in range(Y_SIZE)]


def swap_y(x):
    return lax.ppermute(x, "dp", [(i, i ^ 1) for i in range(Z_SIZE * Y_SIZE)])


def scatter_z(x):
    return lax.psum_scatter(
        x, "dp", scatter_dimension=0, tiled=True, axis_index_groups=z_groups()
    )


def exchange(x):
    return lax.all_to_all(x, "mp", split_axis=0, concat_axis=0, tiled=True)


def add_pair(half, whole, received, first_row, rows):
    def body(half_ref, whole_ref, received_ref, out_ref):
        out_ref[0] = (
            whole_ref[0, 0].astype(jnp.float32) + received_ref[0].astype(jnp.float32)
        ).astype(jnp.bfloat16)

    mats = whole.shape[2]
    per = 8
    return pl.pallas_call(
        body,
        grid_spec=pltpu.PrefetchScalarGridSpec(
            num_scalar_prefetch=1,
            grid=(Z_SIZE, mats // per),
            in_specs=[
                pl.BlockSpec((1, 1, per, rows, HEAD), lambda z, k, h: (z, h[0], k, first_row // rows, 0)),
                pl.BlockSpec((1, per, rows, HEAD), lambda z, k, h: (z, k, 0, 0)),
            ],
            out_specs=pl.BlockSpec((1, per, rows, HEAD), lambda z, k, h: (z, k, 0, 0)),
        ),
        out_shape=jax.ShapeDtypeStruct((Z_SIZE, mats, rows, HEAD), jnp.bfloat16),
        compiler_params=params(),
        name="add_pair",
    )(half, whole, received)


def mix(index, own, received, held, gram, first_row, rows, last):
    mats = own.shape[-3]
    paired = received is not None
    begun = gram is not None

    def body(index_ref, *refs):
        refs = list(refs)
        own_ref = refs.pop(0)
        received_ref = refs.pop(0) if paired else None
        first_ref, second_ref = refs.pop(0), refs.pop(0)
        before_ref = refs.pop(0) if begun else None
        sent_ref, mixed_ref, gram_ref = refs
        k = pl.program_id(0)
        summed = own_ref[...].reshape(rows, HEAD).astype(jnp.float32)
        if paired:
            summed = summed + received_ref[0].astype(jnp.float32)
        rounded = summed.astype(jnp.bfloat16)
        sent_ref[0, 0] = rounded
        summed = rounded.astype(jnp.float32)
        second = index_ref[k] % 2 == 1
        stored = jnp.where(second, second_ref[0].astype(jnp.float32), first_ref[0].astype(jnp.float32))
        renewed = (momentum_rate * stored + summed).astype(jnp.bfloat16)
        mixed = (summed + momentum_rate * renewed.astype(jnp.float32)).astype(jnp.bfloat16)
        mixed_ref[0] = mixed
        part = lax.dot_general(
            mixed, mixed, (((0,), (0,)), ((), ())), preferred_element_type=jnp.float32
        )
        if begun:
            part = part + before_ref[0]
        gram_ref[0] = part.astype(gram_ref.dtype)

    at_row = first_row // rows
    if paired:
        own_spec = pl.BlockSpec((1, 1, rows, HEAD), lambda k, i: (i[mats], k, 0, 0))
    else:
        own_spec = pl.BlockSpec((1, rows, HEAD), lambda k, i: (k, 0, 0))
    in_specs, operands = [own_spec], [own]
    if paired:
        in_specs.append(pl.BlockSpec((1, rows, HEAD), lambda k, i: (k, 0, 0)))
        operands.append(received)
    for one in held:
        in_specs.append(pl.BlockSpec((1, rows, HEAD), lambda k, i: (i[k] // 2, at_row, 0)))
        operands.append(one)
    if begun:
        in_specs.append(pl.BlockSpec((1, HEAD, HEAD), lambda k, i: (k, 0, 0)))
        operands.append(gram)
    return pl.pallas_call(
        body,
        grid_spec=pltpu.PrefetchScalarGridSpec(
            num_scalar_prefetch=1,
            grid=(mats,),
            in_specs=in_specs,
            out_specs=[
                pl.BlockSpec((1, 1, rows, HEAD), lambda k, i: (i[k] // 2, i[k] % 2, 0, 0)),
                pl.BlockSpec((1, rows, HEAD), lambda k, i: (k, 0, 0)),
                pl.BlockSpec((1, HEAD, HEAD), lambda k, i: (k, 0, 0)),
            ],
        ),
        out_shape=[
            jax.ShapeDtypeStruct((held[0].shape[0], 2, rows, HEAD), jnp.bfloat16),
            jax.ShapeDtypeStruct((mats, rows, HEAD), jnp.bfloat16),
            jax.ShapeDtypeStruct((mats, HEAD, HEAD), jnp.bfloat16 if last else jnp.float32),
        ],
        compiler_params=params(),
        name="mix",
    )(index, *operands)


def polynomial(parts):
    count = parts.shape[0]

    def product(a, b):
        return jnp.dot(a, b, preferred_element_type=jnp.float32, precision=lax.Precision.HIGHEST)

    def body(parts_ref, out_ref):
        gram = jnp.sum(parts_ref[...].astype(jnp.float32), axis=0)
        row = lax.broadcasted_iota(jnp.int32, (HEAD, HEAD), 0)
        column = lax.broadcasted_iota(jnp.int32, (HEAD, HEAD), 1)
        unit = jnp.where(row == column, 1.0, 0.0)
        squares = jnp.sum(jnp.sum(gram * unit, axis=0, keepdims=True), axis=1, keepdims=True)
        inverse = 1.0 / (jnp.sqrt(squares) + norm_eps)
        gram = (gram * inverse) * inverse
        turn = None
        for iteration in range(ITERS):
            half = gram.astype(jnp.bfloat16).astype(jnp.float32)
            poly = coef_second * half + coef_third * product(half, half)
            step = coef_first * unit + poly
            if iteration + 1 < ITERS:
                gram = product(step, product(gram, step))
            turn = step if turn is None else product(turn, step)
        turn = turn * (math.sqrt(ROWS) * inverse)
        out_ref[...] = jnp.broadcast_to(turn.astype(jnp.bfloat16)[None], out_ref.shape)

    return pl.pallas_call(
        body,
        out_shape=jax.ShapeDtypeStruct((count, HEAD, HEAD), jnp.bfloat16),
        compiler_params=params(),
        name="polynomial",
    )(parts)


def turn_all(mixed, turns):
    mats = turns.shape[0]
    total = sum(m.shape[1] for m in mixed)

    def body(*refs):
        turn_ref, out_ref = refs[-2], refs[-1]
        at = 0
        for ref in refs[:-2]:
            rows = ref.shape[1]
            out_ref[0, at : at + rows] = jnp.dot(
                ref[0], turn_ref[0], preferred_element_type=jnp.float32
            ).astype(jnp.bfloat16)
            at += rows

    return pl.pallas_call(
        body,
        grid=(mats,),
        in_specs=[pl.BlockSpec((1, m.shape[1], HEAD), lambda k: (k, 0, 0)) for m in mixed]
        + [pl.BlockSpec((1, HEAD, HEAD), lambda k: (k, 0, 0))],
        out_specs=pl.BlockSpec((1, total, HEAD), lambda k: (k, 0, 0)),
        out_shape=jax.ShapeDtypeStruct((mats, total, HEAD), jnp.bfloat16),
        compiler_params=params(),
        name="turn_all",
    )(*mixed, turns)


def renew(filled, stored, arrived):
    slots, sources, total, _ = stored.shape
    per = 4

    def body(filled_ref, stored_ref, *refs):
        out_ref = refs[-1]
        full = filled_ref[pl.program_id(0)] == 1
        at = 0
        for ref in refs[:-1]:
            rows = ref.shape[2]
            here = slice(at, at + rows)
            grad = jnp.where(full, ref[:, 0].astype(jnp.float32), 0.0)
            out_ref[0, :, here] = (
                momentum_rate * stored_ref[0, :, here].astype(jnp.float32) + grad
            ).astype(jnp.bfloat16)
            at += rows

    return pl.pallas_call(
        body,
        grid_spec=pltpu.PrefetchScalarGridSpec(
            num_scalar_prefetch=1,
            grid=(slots, sources // per),
            in_specs=[pl.BlockSpec((1, per, total, HEAD), lambda s, p, f: (s, p, 0, 0))]
            + [
                pl.BlockSpec((per, 1, a.shape[2], HEAD), lambda s, p, f: (p, s, 0, 0))
                for a in arrived
            ],
            out_specs=pl.BlockSpec((1, per, total, HEAD), lambda s, p, f: (s, p, 0, 0)),
        ),
        out_shape=jax.ShapeDtypeStruct(stored.shape, jnp.bfloat16),
        compiler_params=params(),
        name="renew",
    )(filled, stored, *arrived)


def on_device(grads, momentum, owner_table):
    owners = owner_table[0]
    mp_size, slots = owners.shape
    mats = grads.shape[1] // (Z_SIZE * Y_SIZE)
    piece = grads.shape[2]
    me = lax.axis_index("mp")
    half = lax.axis_index("dp") % Y_SIZE
    flat = owners.reshape(-1)
    wanted = jnp.arange(mats, dtype=jnp.int32)
    place = jnp.arange(flat.shape[0], dtype=jnp.int32)
    placed = jnp.sum(jnp.where(flat[None, :] == wanted[:, None], place[None, :], 0), axis=1)
    index = jnp.concatenate([placed, half[None]]).astype(jnp.int32)
    filled = (lax.dynamic_index_in_dim(owners, me, 0, keepdims=False) < mats).astype(jnp.int32)

    own = grads[0].reshape(Z_SIZE, Y_SIZE, mats, piece, HEAD)
    stored = momentum[0, 0].reshape(slots, mp_size, piece, HEAD)

    def chunk(first_row, rows):
        return own[:, :, :, first_row : first_row + rows]

    half_index = half[None].astype(jnp.int32)
    reduced = []
    pending = {}
    for number, (first_row, rows, y_first) in enumerate(CHUNKS):
        if y_first:
            away = lax.dynamic_index_in_dim(chunk(first_row, rows), 1 - half, 1, keepdims=False)
            pending[number] = swap_y(away)
    held = [exchange(stored[s]) for s in range(slots)]
    for number, (first_row, rows, y_first) in enumerate(CHUNKS):
        if y_first:
            paired = add_pair(half_index, own, pending[number], first_row, rows)
            part = scatter_z(paired.reshape(Z_SIZE * mats, rows, HEAD))
            reduced.append((part, None))
        else:
            part = scatter_z(chunk(first_row, rows).reshape(-1, rows, HEAD))
            part = part.reshape(Y_SIZE, mats, rows, HEAD)
            away = lax.dynamic_index_in_dim(part, 1 - half, 0, keepdims=False)
            reduced.append((part, swap_y(away)))

    gram, arrived, mixed = None, [], []
    for number, (first_row, rows, _) in enumerate(CHUNKS):
        part, received = reduced[number]
        last = number + 1 == len(CHUNKS)
        sent, one, gram = mix(index, part, received, held, gram, first_row, rows, last)
        mixed.append(one)
        arrived.append(exchange(sent))
    turns = exchange(polynomial(exchange(gram)))
    update = turn_all(mixed, turns)
    renewed = renew(filled, stored, arrived)
    return (update, renewed.reshape(1, 1, slots, -1, HEAD))


def solution(mesh):
    in_specs = (P("dp", None, "mp", None), P("dp", "mp", None, None, None), P("dp", None, None))
    out_specs = (P("dp", "mp", None), P("dp", "mp", None, None, None))
    return jax.shard_map(
        on_device, mesh=mesh, in_specs=in_specs, out_specs=out_specs, check_vma=False
    )
```

time: 400 us -> 326 us (0.81)
  waiting for transfers between devices: 254 us -> 115 us
  Pallas kernels: 0 us -> 50 us
  blocking collectives: 57.3 us -> 82 us
  other arithmetic: 23.1 us -> 0.38 us
  matrix products: 20.4 us -> 0 us
  starting transfers between devices: 5.37 us -> 23.7 us
  local copies, waits for them, and re-layouts: 26 us -> 37.9 us
    reduce_scatter x1 -> x3, waiting for transfers between devices: 197 us -> 22.8 us  [scatter_z(): lax.psum_scatter(x, 'dp', scatter_dimension=0, tiled=True, axis_index_gro...]
    ppermute x0 -> x3, waiting for transfers between devices: none -> 61.8 us  [swap_y(): return lax.ppermute(x, 'dp', [(i, i ^ 1) for i in range(Z_SIZE * Y_SIZE)])]
    pallas_call x0 -> x7, Pallas kernels: none -> 50 us  [the longest x3 28.3 us: mix(): pl.pallas_call(body, grid_spec=pltpu.PrefetchScalarGridSpec(num_scalar_pr...]
    all_to_all x1 -> x4, blocking collectives: 57.3 us -> 82 us  [exchange(): return lax.all_to_all(x, 'mp', split_axis=0, concat_axis=0, tiled=True)]
    all_to_all x1 -> x3, waiting for transfers between devices: 55.6 us -> 30.8 us  [exchange(): return lax.all_to_all(x, 'mp', split_axis=0, concat_axis=0, tiled=True)]
    dot_general x4 -> x0, matrix products: 20.4 us -> none  [the longest x2 14.1 us: iterate_all(): jnp.einsum('mrh,mhk->mrk', iterate, poly, preferred_element_type=jnp.floa...]
    slice x0 -> x3, local copies, waits for them, and re-layouts: none -> 17.8 us  [the longest x2 14 us: chunk(): return own[:, :, :, first_row:first_row + rows]]
    convert_element_type x3 -> x1, other arithmetic: 16.5 us -> 0.18 us  [on_device(): (lax.dynamic_index_in_dim(owners, me, 0, keepdims=False) < mats).astype(j...]
  transfers between devices with their start and end apart: 2 -> 9, of which waited for: 2 -> 5; matrix products, arithmetic and copies ran while one was open for 0% -> 5% of each run, Pallas kernels for 0% -> 10%
where the time goes in v1:
time: 326 us; the launch traced here: 323 us
  waiting for transfers between devices  115 us (35%)
  blocking collectives  82 us (25%)
  Pallas kernels  50 us (15%)
  local copies, waits for them, and re-layouts  37.9 us (12%)
  starting transfers between devices  23.7 us (7%)
  between operations  13.9 us (4%)
    all_to_all x4, blocking collectives, exchange(): return lax.all_to_all(x, 'mp', split_axis=0, concat_axis=0, tiled=True)  82 us
    ppermute x3, waiting for transfers between devices, swap_y(): return lax.ppermute(x, 'dp', [(i, i ^ 1) for i in range(Z_SIZE * Y_SIZE)])  61.8 us
    all_to_all x3, waiting for transfers between devices, exchange(): return lax.all_to_all(x, 'mp', split_axis=0, concat_axis=0, tiled=True)  30.8 us
    pallas_call x3, Pallas kernels, mix(): pl.pallas_call(body, grid_spec=pltpu.PrefetchScalarGridSpec(num_scalar_pr...  28.3 us
    reduce_scatter x3, waiting for transfers between devices, scatter_z(): lax.psum_scatter(x, 'dp', scatter_dimension=0, tiled=True, axis_index_gro...  22.8 us
    unnamed x39, local copies, waits for them, and re-layouts  14.8 us
    all_to_all x3, starting transfers between devices, exchange(): return lax.all_to_all(x, 'mp', split_axis=0, concat_axis=0, tiled=True)  14.3 us
    slice x2, local copies, waits for them, and re-layouts, chunk(): return own[:, :, :, first_row:first_row + rows]  14 us
  transfers between devices with their start and end apart: 9, of which 5 were waited for; matrix products, arithmetic and copies ran while one was open for 5% of the time, Pallas kernels for 10%

profile of v1, /device:TPU:1, one launch (start us, length us, event | category | flops | bytes accessed | tf_op | source)
XLA Modules:
  0.0 323.3 jit_solution(15139757507041393141)
XLA Ops:
  7.2 7.8 %slice.22 = bf16[4,2,16,256,128]{4,3,2,1,0:T(8,128)(2,1)} slice(bf16[4,2,16,512,128]{4,3,2,1,0:T(8,128)(2,1)} %bitcast.19), slice={[0:4], [0:2], [0:16], [0:256], [0:128]} | slice | bytes 16777216 | tf_op jit(solution)/shard_map/slice | solution.py:253
  15.1 6.2 %fusion.1 = (bf16[4,2,16,128,128]{4,3,2,1,0:T(8,128)(2,1)}, bf16[4,2,16,128,128]{4,3,2,1,0:T(8,128)(2,1)}) fusion(bf16[4,2,16,512,128]{4,3,2,1,0:T(8,128)(2,1)} %bitcast.20), kind=kLoop, calls=%fused_computation.8 | loop fusion | bytes 16777216 | tf_op jit(solution)/shard_map/slice | solution.py:253
  21.3 1.7 dynamic-slice_bitcast_fusion
  23.1 3.8 %collective-permute-start.2 = (bf16[4,16,128,128]{3,2,1,0:T(8,128)(2,1)S(1)}, bf16[4,16,128,128]{3,2,1,0:T(8,128)(2,1)S(1)}, u32[]{:S(2)}, u32[]{:S(2)}) collective-permute-start(bf16[4,16,128,128]{3,2,1,0:T(8,128)(2,1)S(1)} %dynamic-slice_bitcast_fusion), channel_id=1, source_target_pairs={{0,16},{16,0},{32,48},{48,32},{64,80},{80,64},{96,112},{112,96},{1... | collective-permute-start | bytes 6291464 | tf_op jit(solution)/shard_map/ppermute | solution.py:35
  26.9 45.1 %collective-permute-done.2.received_ref = bf16[4,16,128,128]{3,2,1,0:T(8,128)(2,1)S(1)} collective-permute-done((bf16[4,16,128,128]{3,2,1,0:T(8,128)(2,1)S(1)}, bf16[4,16,128,128]{3,2,1,0:T(8,128)(2,1)S(1)}, u32[]{:S(2)}, u32[]{:S(2)}) %collective-permute-start.2) | collective-permute-done | bytes 2097184 | tf_op jit(solution)/shard_map/ppermute | solution.py:35
  72.0 5.8 %add_pair.1 = bf16[4,16,128,128]{3,2,1,0:T(8,128)(2,1)} custom-call(s32[1]{0:T(128)} %bitcast.half_ref, bf16[4,2,16,512,128]{4,3,2,1,0:T(8,128)(2,1)} %bitcast.21, bf16[4,16,128,128]{3,2,1,0:T(8,128)(2,1)S(1)} %collective-permute-done.2.received_ref), custom_call_target="tpu_custom_call" | custom-call | tf_op jit(solution)/shard_map/add_pair/pallas_call | solution.py:56
  77.8 3.9 %fusion.2 = (bf16[1,1,1,8192,128]{4,3,2,1,0:T(8,128)(2,1)}, bf16[1,1,1,8192,128]{4,3,2,1,0:T(8,128)(2,1)S(1)}) fusion(bf16[1,1,2,8192,128]{4,3,2,1,0:T(8,128)(2,1)} %param.4), kind=kLoop, calls=%fused_computation.9 | loop fusion | bytes 8388608 | tf_op jit(solution)/shard_map/slice | solution.py:262
  81.7 33.5 %all_to_all.35.refs_2_.refs_1_ = bf16[16,512,128]{2,1,0:T(8,128)(2,1)} all-to-all(bf16[16,512,128]{2,1,0:T(8,128)(2,1)S(1)} %bitcast.25), channel_id=1, replica_groups=mesh['dp'=8,'mp'=16] {'mp'}, dimensions={0} | all-to-all | bytes 4194304 | tf_op jit(solution)/shard_map/all_to_all | solution.py:45
  115.2 5.3 %all-to-all-start.1 = ((bf16[16,512,128]{2,1,0:T(8,128)(2,1)}), bf16[16,512,128]{2,1,0:T(8,128)(2,1)}, u32[]{:S(2)}, u32[]{:S(2)}) async-start(bf16[16,512,128]{2,1,0:T(8,128)(2,1)} %bitcast.6), calls=%async_computation.2 | async-start | bytes 4194304 | tf_op jit(solution)/shard_map/all_to_all | solution.py:45
  120.5 2.3 dynamic-slice_bitcast_fusion.1
  122.9 2.6 collective-permute-start
  125.5 22.7 %reduce-scatter.6.cloned.1.call-done = bf16[32,128,128]{2,1,0:T(8,128)(2,1)} async-done(((bf16[128,128,128]{2,1,0:T(8,128)(2,1)}), bf16[32,128,128]{2,1,0:T(8,128)(2,1)}) %reduce-scatter.6.cloned.1.call-update) | async-done | bytes 1048592 | tf_op jit(solution)/shard_map/reduce_scatter | solution.py:39
  148.2 1.1 dynamic-slice_bitcast_fusion.2
  149.3 2.8 collective-permute-start.1
  152.5 16.7 %collective-permute-done.refs_1_ = bf16[16,256,128]{2,1,0:T(8,128)(2,1)S(1)} collective-permute-done((bf16[16,256,128]{2,1,0:T(8,128)(2,1)}, bf16[16,256,128]{2,1,0:T(8,128)(2,1)S(1)}, u32[]{:S(2)}, u32[]{:S(2)}) %collective-permute-start) | collective-permute-done | bytes 1048608 | tf_op jit(solution)/shard_map/ppermute | solution.py:35
  169.2 10.5 %mix.3 = (bf16[16,2,256,128]{3,2,1,0:T(8,128)(2,1)S(1)}, bf16[16,256,128]{2,1,0:T(8,128)(2,1)S(1)}, f32[16,128,128]{2,1,0:T(8,128)S(1)}) custom-call(s32[17]{0:T(128)S(1)} %pad_add_fusion.index_ref, bf16[2,16,256,128]{3,2,1,0:T(8,128)(2,1)} %bitcast.27, bf16[16,256,128]{2,1,0:T(8,128)(2,1)S(1)} %collective-permute-done.refs_1_, ...), custom_call_target="tpu_custom_call" | custom-call | tf_op jit(solution)/shard_map/mix/pallas_call | solution.py:119
  179.6 1.3 copy-done.5
  183.8 9.1 %mix.4 = (bf16[16,2,128,128]{3,2,1,0:T(8,128)(2,1)S(1)}, bf16[16,128,128]{2,1,0:T(8,128)(2,1)S(1)}, f32[16,128,128]{2,1,0:T(8,128)S(1)}) custom-call(s32[17]{0:T(128)S(1)} %pad_add_fusion.index_ref, bf16[2,16,128,128]{3,2,1,0:T(8,128)(2,1)S(1)} %bitcast.18, bf16[16,128,128]{2,1,0:T(8,128)(2,1)S(1)} %copy-done.17, ...), custom_call_target="tpu_custom_call" | custom-call | tf_op jit(solution)/shard_map/mix/pallas_call | solution.py:119
  195.7 1.2 copy-done.10
  197.9 8.7 %mix.5 = (bf16[16,2,128,128]{3,2,1,0:T(8,128)(2,1)S(1)}, bf16[16,128,128]{2,1,0:T(8,128)(2,1)S(1)}, bf16[16,128,128]{2,1,0:T(8,128)(2,1)S(1)}) custom-call(s32[17]{0:T(128)S(1)} %pad_add_fusion.index_ref, bf16[16,128,128]{2,1,0:T(8,128)(2,1)S(1)} %copy-done.11, bf16[16,512,128]{2,1,0:T(8,128)(2,1)S(1)} %copy-done, ...), custom_call_target="tpu_custom_call" | custom-call | tf_op jit(solution)/shard_map/mix/pallas_call | solution.py:119
  206.7 15.6 %all_to_all.36.parts_ref = bf16[16,128,128]{2,1,0:T(8,128)(2,1)S(1)} all-to-all(bf16[16,128,128]{2,1,0:T(8,128)(2,1)S(1)} %get-tuple-element.16), channel_id=1, replica_groups=mesh['dp'=8,'mp'=16] {'mp'}, dimensions={0} | all-to-all | bytes 1048576 | tf_op jit(solution)/shard_map/all_to_all | solution.py:45
  222.3 19.1 %all_to_all.37.refs_2_ = bf16[16,2,128,128]{3,2,1,0:T(8,128)(2,1)S(1)} all-to-all(bf16[16,2,128,128]{3,2,1,0:T(8,128)(2,1)S(1)} %get-tuple-element.19), channel_id=1, replica_groups=mesh['dp'=8,'mp'=16] {'mp'}, dimensions={0} | all-to-all | bytes 2097152 | tf_op jit(solution)/shard_map/all_to_all | solution.py:45
  241.4 4.5 %all-to-all-start.5 = ((bf16[16,2,128,128]{3,2,1,0:T(8,128)(2,1)}), bf16[16,2,128,128]{3,2,1,0:T(8,128)(2,1)S(1)}, u32[]{:S(2)}, u32[]{:S(2)}) async-start(bf16[16,2,128,128]{3,2,1,0:T(8,128)(2,1)} %copy-done.6), calls=%async_computation.8 | async-start | bytes 2097152 | tf_op jit(solution)/shard_map/all_to_all | solution.py:45
  245.9 1.3 polynomial.1
  247.2 14.6 %all-to-all-done.5.refs_1_ = bf16[16,2,128,128]{3,2,1,0:T(8,128)(2,1)S(1)} async-done(((bf16[16,2,128,128]{3,2,1,0:T(8,128)(2,1)}), bf16[16,2,128,128]{3,2,1,0:T(8,128)(2,1)S(1)}, u32[]{:S(2)}, u32[]{:S(2)}) %all-to-all-start.5) | async-done | bytes 1048608 | tf_op jit(solution)/shard_map/all_to_all | solution.py:45
  261.9 13.8 %all_to_all.38.refs_3_ = bf16[16,128,128]{2,1,0:T(8,128)(2,1)} all-to-all(bf16[16,128,128]{2,1,0:T(8,128)(2,1)S(1)} %polynomial.1), channel_id=1, replica_groups=mesh['dp'=8,'mp'=16] {'mp'}, dimensions={0} | all-to-all | bytes 1048576 | tf_op jit(solution)/shard_map/all_to_all | solution.py:45
  275.7 4.6 %all-to-all-start.4 = ((bf16[16,2,256,128]{3,2,1,0:T(8,128)(2,1)}), bf16[16,2,256,128]{3,2,1,0:T(8,128)(2,1)S(1)}, u32[]{:S(2)}, u32[]{:S(2)}) async-start(bf16[16,2,256,128]{3,2,1,0:T(8,128)(2,1)} %copy-done.5), calls=%async_computation.7 | async-start | bytes 4194304 | tf_op jit(solution)/shard_map/all_to_all | solution.py:45
  281.5 1.2 copy-done.8
  284.8 6.8 %turn_all.1 = bf16[16,512,128]{2,1,0:T(8,128)(2,1)} custom-call(bf16[16,256,128]{2,1,0:T(8,128)(2,1)S(1)} %copy-done.8, bf16[16,128,128]{2,1,0:T(8,128)(2,1)S(1)} %copy-done.13, bf16[16,128,128]{2,1,0:T(8,128)(2,1)S(1)} %copy-done.15, bf16[16,128,128]{2,1,0:T(8,128)(2,1)S(1)} %copy-done.4), custom_call_target="tpu_custom_call" | custom-call | tf_op jit(solution)/shard_map/turn_all/pallas_call | solution.py:188
  291.6 16.2 %all-to-all-done.4.refs_0_ = bf16[16,2,256,128]{3,2,1,0:T(8,128)(2,1)S(1)} async-done(((bf16[16,2,256,128]{3,2,1,0:T(8,128)(2,1)}), bf16[16,2,256,128]{3,2,1,0:T(8,128)(2,1)S(1)}, u32[]{:S(2)}, u32[]{:S(2)}) %all-to-all-start.4) | async-done | bytes 2097184 | tf_op jit(solution)/shard_map/all_to_all | solution.py:45
  307.8 1.2 copy-done.2
  309.0 7.7 %renew.1 = bf16[2,16,512,128]{3,2,1,0:T(8,128)(2,1)} custom-call(s32[2]{0:T(128)S(1)} %fusion.filled_ref, bf16[2,16,512,128]{3,2,1,0:T(8,128)(2,1)} %bitcast.23, bf16[16,2,256,128]{3,2,1,0:T(8,128)(2,1)S(1)} %all-to-all-done.4.refs_0_, bf16[16,2,128,128]{3,2,1,0:T(8,128)(2,1)S(1)} %copy-done.2, bf16[16,2,128,128]{3,2,1,0:T(8,128)(2,1)S(1)} %all_to_all.37.refs_2_), custom_call_target="tpu_custom_call" | custom-call | tf_op jit(solution)/shard_map/renew/pallas_call | solution.py:217
  (49 shorter events, 10.5 us)
Async XLA Ops:
  7.2 113.3 %reduce-scatter.4.cloned.1.call-start = ((), (), s32[]{:S(2)}) async-start(), calls=%async_computation.10 | async-start | bytes 10485760 | tf_op jit(solution)/shard_map/reduce_scatter | solution.py:39
  15.0 133.2 %reduce-scatter.6.cloned.1.call-start = ((), (), s32[]{:S(2)}) async-start(), calls=%async_computation.11 | async-start | bytes 5242880 | tf_op jit(solution)/shard_map/reduce_scatter | solution.py:39
  21.3 174.4 %reduce-scatter.8.cloned.1.call-start = ((), (), s32[]{:S(2)}) async-start(), calls=%async_computation.12 | async-start | bytes 2621440 | tf_op jit(solution)/shard_map/reduce_scatter | solution.py:39
  23.1 48.9 %collective-permute-start.2 = (bf16[4,16,128,128]{3,2,1,0:T(8,128)(2,1)S(1)}, bf16[4,16,128,128]{3,2,1,0:T(8,128)(2,1)S(1)}, u32[]{:S(2)}, u32[]{:S(2)}) collective-permute-start(bf16[4,16,128,128]{3,2,1,0:T(8,128)(2,1)S(1)} %dynamic-slice_bitcast_fusion), channel_id=1, source_target_pairs={{0,16},{16,0},{32,48},{48,32},{64,80},{80,64},{96,112},{112,96},{1... | collective-permute-start | bytes 6291464 | tf_op jit(solution)/shard_map/ppermute | solution.py:35
  115.2 37.2 %all-to-all-start.1 = ((bf16[16,512,128]{2,1,0:T(8,128)(2,1)}), bf16[16,512,128]{2,1,0:T(8,128)(2,1)}, u32[]{:S(2)}, u32[]{:S(2)}) async-start(bf16[16,512,128]{2,1,0:T(8,128)(2,1)} %bitcast.6), calls=%async_computation.2 | async-start | bytes 4194304 | tf_op jit(solution)/shard_map/all_to_all | solution.py:45
  120.5 31.6 %copy-start.18 = (s32[1,16,2]{1,2,0:T(2,128)S(1)}, s32[1,16,2]{1,2,0:T(2,128)}, u32[]{:S(2)}) copy-start(s32[1,16,2]{1,2,0:T(2,128)} %param.5) | copy-start | bytes 388
  122.9 46.3 %collective-permute-start = (bf16[16,256,128]{2,1,0:T(8,128)(2,1)}, bf16[16,256,128]{2,1,0:T(8,128)(2,1)S(1)}, u32[]{:S(2)}, u32[]{:S(2)}) collective-permute-start(bf16[16,256,128]{2,1,0:T(8,128)(2,1)} %dynamic-slice_bitcast_fusion.1), channel_id=1, source_target_pairs={{0,16},{16,0},{32,48},{48,32},{64,80},{80,64},{96,112},{112,96},{1... | collective-permute-start | bytes 3145736 | tf_op jit(solution)/shard_map/ppermute | solution.py:35
  149.3 32.7 %collective-permute-start.1 = (bf16[16,128,128]{2,1,0:T(8,128)(2,1)S(1)}, bf16[16,128,128]{2,1,0:T(8,128)(2,1)S(1)}, u32[]{:S(2)}, u32[]{:S(2)}) collective-permute-start(bf16[16,128,128]{2,1,0:T(8,128)(2,1)S(1)} %dynamic-slice_bitcast_fusion.2), channel_id=1, source_target_pairs={{0,16},{16,0},{32,48},{48,32},{64,80},{80,64},{96,112},{112,96},{1... | collective-permute-start | bytes 1572872 | tf_op jit(solution)/shard_map/ppermute | solution.py:35
  152.5 30.3 %copy-start.3 = (bf16[32,128,128]{2,1,0:T(8,128)(2,1)S(1)}, bf16[32,128,128]{2,1,0:T(8,128)(2,1)}, u32[]{:S(2)}) copy-start(bf16[32,128,128]{2,1,0:T(8,128)(2,1)} %reduce-scatter.6.cloned.1.call-done) | copy-start | bytes 3145732
  179.6 1.3 copy-start.5
  181.0 1.0 copy-start.7
  181.9 0.8 copy-start.16
  182.8 1.0 copy-start.17
  183.8 11.9 %copy-start = (bf16[16,512,128]{2,1,0:T(8,128)(2,1)S(1)}, bf16[16,512,128]{2,1,0:T(8,128)(2,1)}, u32[]{:S(2)}) copy-start(bf16[16,512,128]{2,1,0:T(8,128)(2,1)} %all_to_all.35.refs_2_.refs_1_) | copy-start | bytes 6291460
  192.9 1.0 copy-start.6
  193.9 1.0 copy-start.9
  194.8 0.8 copy-start.12
  195.7 1.2 copy-start.10
  196.9 1.0 copy-start.11
  206.7 34.8 %copy-start.14 = (bf16[16,128,128]{2,1,0:T(8,128)(2,1)}, bf16[16,128,128]{2,1,0:T(8,128)(2,1)S(1)}, u32[]{:S(2)}) copy-start(bf16[16,128,128]{2,1,0:T(8,128)(2,1)S(1)} %get-tuple-element.15.refs_2_) | copy-start | bytes 1572868
  241.4 20.5 %all-to-all-start.5 = ((bf16[16,2,128,128]{3,2,1,0:T(8,128)(2,1)}), bf16[16,2,128,128]{3,2,1,0:T(8,128)(2,1)S(1)}, u32[]{:S(2)}, u32[]{:S(2)}) async-start(bf16[16,2,128,128]{3,2,1,0:T(8,128)(2,1)} %copy-done.6), calls=%async_computation.8 | async-start | bytes 2097152 | tf_op jit(solution)/shard_map/all_to_all | solution.py:45
  261.9 13.8 %copy-start.1 = (bf16[16,2,128,128]{3,2,1,0:T(8,128)(2,1)}, bf16[16,2,128,128]{3,2,1,0:T(8,128)(2,1)S(1)}, u32[]{:S(2)}) copy-start(bf16[16,2,128,128]{3,2,1,0:T(8,128)(2,1)S(1)} %all-to-all-done.5.refs_1_) | copy-start | bytes 3145732
  275.7 32.1 %all-to-all-start.4 = ((bf16[16,2,256,128]{3,2,1,0:T(8,128)(2,1)}), bf16[16,2,256,128]{3,2,1,0:T(8,128)(2,1)S(1)}, u32[]{:S(2)}, u32[]{:S(2)}) async-start(bf16[16,2,256,128]{3,2,1,0:T(8,128)(2,1)} %copy-done.5), calls=%async_computation.7 | async-start | bytes 4194304 | tf_op jit(solution)/shard_map/all_to_all | solution.py:45
  280.4 1.0 copy-start.4
  281.4 1.2 copy-start.8
  282.7 1.0 copy-start.13
  283.7 1.0 copy-start.15
  307.8 1.2 copy-start.2
Sparse Core Ops, SparseCore 0:
  15.1 83.9 reduce-scatter.3
  101.6 46.5 reduce-scatter.5
  151.3 29.4 reduce-scatter.7

commit v2 on v1

v2 whole, which is shorter than its diff:
```python
import math

import jax
import jax.numpy as jnp
from jax import lax
from jax.experimental import pallas as pl
from jax.experimental.pallas import tpu as pltpu
from jax.sharding import PartitionSpec as P

ROWS = 8192
HEAD = 128
ITERS = 2

momentum_rate = 0.95
coef_first = 3.4445
coef_second = -4.775
coef_third = 2.0315
norm_eps = 1e-07

Z_SIZE = 4
Y_SIZE = 2
EARLY, PAIRED, LATE = (256, 256), (192, 64), (0, 192)
SOON = (192, 320)
VMEM = 48 * 1024 * 1024


def params():
    return pltpu.CompilerParams(vmem_limit_bytes=VMEM)


def z_groups():
    return [[z * Y_SIZE + y for z in range(Z_SIZE)] for y in range(Y_SIZE)]


def swap_y(x):
    return lax.ppermute(x, "dp", [(i, i ^ 1) for i in range(Z_SIZE * Y_SIZE)])


def scatter_z(x):
    return lax.psum_scatter(
        x, "dp", scatter_dimension=0, tiled=True, axis_index_groups=z_groups()
    )


def barrier(*values):
    return lax.optimization_barrier(values)


def exchange(x):
    return lax.all_to_all(x, "mp", split_axis=0, concat_axis=0, tiled=True)


def shift_z(x, by):
    pairs = [
        (z * Y_SIZE + y, (z + by) % Z_SIZE * Y_SIZE + y) for z in range(Z_SIZE) for y in range(Y_SIZE)
    ]
    return lax.ppermute(x, "dp", pairs)


def whole(*shape):
    return pl.BlockSpec(shape, lambda n, i: (0,) * len(shape))


def add_pair(place, own, received, first_row, rows):
    mats = own.shape[2]

    def body(place_ref, own_ref, received_ref, out_ref):
        out_ref[0] = (
            own_ref[0, 0].astype(jnp.float32) + received_ref[0].astype(jnp.float32)
        ).astype(jnp.bfloat16)

    return pl.pallas_call(
        body,
        grid_spec=pltpu.PrefetchScalarGridSpec(
            num_scalar_prefetch=1,
            grid=(Z_SIZE,),
            in_specs=[
                pl.BlockSpec(
                    (1, 1, mats, rows, HEAD), lambda z, i: (z, i[0], 0, first_row // rows, 0)
                ),
                pl.BlockSpec((1, mats, rows, HEAD), lambda z, i: (z, 0, 0, 0)),
            ],
            out_specs=pl.BlockSpec((1, mats, rows, HEAD), lambda z, i: (z, 0, 0, 0)),
        ),
        out_shape=jax.ShapeDtypeStruct((Z_SIZE, mats, rows, HEAD), jnp.bfloat16),
        compiler_params=params(),
        name="add_pair",
    )(place, own, received)


def mix(index, pieces, held, gram, last):
    mats = index.shape[0] - 2
    owners, piece = held[0].shape[:2]
    begun = gram is not None
    total = sum(rows for _, rows, _ in pieces)
    base = min(first_row for first_row, _, _ in pieces)
    lead = HEAD if last else 0
    terms = [term for _, _, group in pieces for term in group]

    def body(index_ref, *refs):
        refs = list(refs)
        term_refs = [refs.pop(0) for _ in terms]
        held_refs = [refs.pop(0) for _ in held]
        before_ref = refs.pop(0) if begun else None
        sent_ref, mixed_ref = refs[:2]
        for k in range(mats):
            owner, slot = index_ref[2 + k] // 2, index_ref[2 + k] % 2
            part = before_ref[k] if begun else None
            unread = list(zip(term_refs, terms))
            for first_row, rows, group in pieces:
                here, unread = unread[: len(group)], unread[len(group) :]
                summed = sum(
                    (ref[0, k] if isinstance(term, tuple) else ref[k]).astype(jnp.float32)
                    for ref, term in here
                )
                rounded = summed.astype(jnp.bfloat16)
                start = pl.multiple_of(lead + first_row - base + slot * total, 16)
                sent_ref[owner, pl.ds(start, rows)] = rounded
                summed = rounded.astype(jnp.float32)
                first, second = (ref[owner, first_row : first_row + rows] for ref in held_refs)
                stored = jnp.where(slot == 1, second.astype(jnp.float32), first.astype(jnp.float32))
                renewed = (momentum_rate * stored + summed).astype(jnp.bfloat16)
                mixed = (summed + momentum_rate * renewed.astype(jnp.float32)).astype(jnp.bfloat16)
                mixed_ref[k, first_row - base : first_row - base + rows] = mixed
                product = lax.dot_general(
                    mixed, mixed, (((0,), (0,)), ((), ())), preferred_element_type=jnp.float32
                )
                part = product if part is None else part + product
            if last:
                sent_ref[k, :HEAD] = part.astype(jnp.bfloat16)
            else:
                refs[2][k] = part

    in_specs, operands = [], []
    for first_row, rows, group in pieces:
        for term in group:
            if isinstance(term, tuple):
                in_specs.append(
                    pl.BlockSpec((1, mats, rows, HEAD), lambda n, i, at=term[1]: (i[at], 0, 0, 0))
                )
                operands.append(term[0])
            else:
                in_specs.append(whole(mats, rows, HEAD))
                operands.append(term)
    for one in held:
        in_specs.append(whole(owners, piece, HEAD))
        operands.append(one)
    if begun:
        in_specs.append(whole(mats, HEAD, HEAD))
        operands.append(gram)
    shapes = [
        jax.ShapeDtypeStruct((owners, lead + 2 * total, HEAD), jnp.bfloat16),
        jax.ShapeDtypeStruct((mats, total, HEAD), jnp.bfloat16),
    ]
    if not last:
        shapes.append(jax.ShapeDtypeStruct((mats, HEAD, HEAD), jnp.float32))
    return pl.pallas_call(
        body,
        grid_spec=pltpu.PrefetchScalarGridSpec(
            num_scalar_prefetch=1,
            grid=(1,),
            in_specs=in_specs,
            out_specs=[whole(*shape.shape) for shape in shapes],
        ),
        out_shape=shapes,
        compiler_params=params(),
        name="mix",
    )(index, *operands)


def polynomial(parts):
    count = parts.shape[0]

    def product(a, b):
        return jnp.dot(a, b, preferred_element_type=jnp.float32, precision=lax.Precision.HIGHEST)

    def body(parts_ref, out_ref):
        gram = jnp.sum(parts_ref[...].astype(jnp.float32), axis=0)
        row = lax.broadcasted_iota(jnp.int32, (HEAD, HEAD), 0)
        column = lax.broadcasted_iota(jnp.int32, (HEAD, HEAD), 1)
        unit = jnp.where(row == column, 1.0, 0.0)
        squares = jnp.sum(jnp.sum(gram * unit, axis=0, keepdims=True), axis=1, keepdims=True)
        inverse = 1.0 / (jnp.sqrt(squares) + norm_eps)
        gram = (gram * inverse) * inverse
        turn = None
        for iteration in range(ITERS):
            half = gram.astype(jnp.bfloat16).astype(jnp.float32)
            poly = coef_second * half + coef_third * product(half, half)
            step = coef_first * unit + poly
            if iteration + 1 < ITERS:
                gram = product(step, product(gram, step))
            turn = step if turn is None else product(turn, step)
        turn = turn * (math.sqrt(ROWS) * inverse)
        out_ref[...] = jnp.broadcast_to(turn.astype(jnp.bfloat16)[None], out_ref.shape)

    return pl.pallas_call(
        body,
        grid=(1,),
        in_specs=[pl.BlockSpec((count, HEAD, HEAD), lambda n: (0, 0, 0))],
        out_specs=pl.BlockSpec((count, HEAD, HEAD), lambda n: (0, 0, 0)),
        out_shape=jax.ShapeDtypeStruct((count, HEAD, HEAD), jnp.bfloat16),
        compiler_params=params(),
        name="polynomial",
    )(parts)


def turn_all(late, soon, turns):
    mats = turns.shape[0]
    piece = LATE[1] + SOON[1]
    per = 2

    def body(late_ref, soon_ref, turn_ref, out_ref):
        for k in range(per):
            for ref, (first_row, rows) in ((late_ref, LATE), (soon_ref, SOON)):
                out_ref[k, first_row : first_row + rows] = jnp.dot(
                    ref[k], turn_ref[k], preferred_element_type=jnp.float32
                ).astype(jnp.bfloat16)

    def block(rows):
        return pl.BlockSpec((per, rows, HEAD), lambda k: (k, 0, 0))

    return pl.pallas_call(
        body,
        grid=(mats // per,),
        in_specs=[block(LATE[1]), block(SOON[1]), block(HEAD)],
        out_specs=block(piece),
        out_shape=jax.ShapeDtypeStruct((mats, piece, HEAD), jnp.bfloat16),
        compiler_params=params(),
        name="turn_all",
    )(late, soon, turns)


def renew(filled, stored, arrived, done, first_row, rows):
    slots, sources, _, _ = stored.shape
    lead = arrived.shape[1] - slots * rows
    unit = math.gcd(first_row, rows)
    per = 8

    def body(filled_ref, stored_ref, arrived_ref, *refs):
        out_ref = refs[-1]
        at = pl.program_id(1) * unit
        for slot in range(slots):
            start = pl.multiple_of(lead + slot * rows + at, 16)
            grad = arrived_ref[:, pl.ds(start, unit)].astype(jnp.float32)
            grad = jnp.where(filled_ref[slot] == 1, grad, 0.0)
            out_ref[slot] = (
                momentum_rate * stored_ref[slot].astype(jnp.float32) + grad
            ).astype(jnp.bfloat16)

    here = pl.BlockSpec((slots, per, unit, HEAD), lambda p, r, f: (0, p, first_row // unit + r, 0))
    return pl.pallas_call(
        body,
        grid_spec=pltpu.PrefetchScalarGridSpec(
            num_scalar_prefetch=1,
            grid=(sources // per, rows // unit),
            in_specs=[here, pl.BlockSpec((per, lead + slots * rows, HEAD), lambda p, r, f: (p, 0, 0))]
            + [pl.BlockSpec(memory_space=pl.ANY)] * (done is not None),
            out_specs=here,
        ),
        out_shape=jax.ShapeDtypeStruct(stored.shape, jnp.bfloat16),
        input_output_aliases={3: 0} if done is not None else {},
        compiler_params=params(),
        name="renew",
    )(filled, stored, arrived, *([done] if done is not None else []))


def on_device(grads, momentum, owner_table):
    owners = owner_table[0]
    mp_size, slots = owners.shape
    mats = grads.shape[1] // (Z_SIZE * Y_SIZE)
    piece = grads.shape[2]
    me = lax.axis_index("mp")
    place = lax.axis_index("dp")
    level, half = place // Y_SIZE, place % Y_SIZE
    flat = owners.reshape(-1)
    wanted = jnp.arange(mats, dtype=jnp.int32)
    position = jnp.arange(flat.shape[0], dtype=jnp.int32)
    placed = jnp.sum(jnp.where(flat[None, :] == wanted[:, None], position[None, :], 0), axis=1)
    place = jnp.stack([half, level]).astype(jnp.int32)
    index = jnp.concatenate([place, placed.astype(jnp.int32)])
    filled = (lax.dynamic_index_in_dim(owners, me, 0, keepdims=False) < mats).astype(jnp.int32)

    own = grads[0].reshape(Z_SIZE, Y_SIZE, mats, piece, HEAD)
    stored = momentum[0, 0].reshape(slots, mp_size, piece, HEAD)

    def half_away(part):
        return lax.dynamic_index_in_dim(part, 1 - half, 0, keepdims=False)

    def rows_of(array, chunk):
        first_row, rows = chunk
        return array[:, :, :, first_row : first_row + rows]

    away, own1 = barrier(
        lax.dynamic_index_in_dim(rows_of(own, PAIRED), 1 - half, 1, keepdims=False), own
    )
    early, own2 = barrier(rows_of(own1, EARLY), own1)
    late = rows_of(own2, LATE)
    early, late = (
        scatter_z(part.reshape(-1, part.shape[3], HEAD)).reshape(Y_SIZE, mats, -1, HEAD)
        for part in (early, late)
    )
    received, later = barrier(swap_y(away), stored[1])
    paired, later = barrier(add_pair(place, own, received, *PAIRED), later)
    held = [exchange(stored[0]), exchange(later)]
    shifted = [
        shift_z(lax.dynamic_index_in_dim(paired, (level + by) % Z_SIZE, 0, keepdims=False), by)
        for by in range(1, Z_SIZE)
    ]
    sent, mixed_soon, gram = mix(
        index,
        [
            (*EARLY, [(early, 0), swap_y(half_away(early))]),
            (*PAIRED, [(paired, 1), *shifted]),
        ],
        held,
        None,
        False,
    )
    late, _ = barrier(late, sent)
    renewed = renew(filled, stored, exchange(sent), None, *SOON)
    renewed, received = barrier(renewed, swap_y(half_away(late)))
    sent, mixed_late = mix(index, [(*LATE, [(late, 0), received])], held, gram, True)
    arrived = exchange(sent)
    turns = exchange(polynomial(arrived))
    renewed = renew(filled, stored, arrived, renewed, *LATE)
    update = turn_all(mixed_late, mixed_soon, turns)
    return (update, renewed.reshape(1, 1, slots, -1, HEAD))


def solution(mesh):
    in_specs = (P("dp", None, "mp", None), P("dp", "mp", None, None, None), P("dp", None, None))
    out_specs = (P("dp", "mp", None), P("dp", "mp", None, None, None))
    return jax.shard_map(
        on_device, mesh=mesh, in_specs=in_specs, out_specs=out_specs, check_vma=False
    )
```

time: 326 us -> 269 us (0.83)
  blocking collectives: 82 us -> 33.7 us
  Pallas kernels: 50 us -> 31 us
  waiting for transfers between devices: 115 us -> 129 us
  local copies, waits for them, and re-layouts: 37.9 us -> 28.9 us
  starting transfers between devices: 23.7 us -> 30.9 us
    all_to_all x4 -> x1, blocking collectives: 82 us -> 33.7 us  [exchange(): return lax.all_to_all(x, 'mp', split_axis=0, concat_axis=0, tiled=True)]
    ppermute x0 -> x3, waiting for transfers between devices: none -> 17.6 us  [shift_z(): return lax.ppermute(x, 'dp', pairs)]
    pallas_call x3 -> x2, Pallas kernels: 28.3 us -> 11.1 us  [mix(): pl.pallas_call(body, grid_spec=pltpu.PrefetchScalarGridSpec(num_scalar_pr...]
    all_to_all x3 -> x4, waiting for transfers between devices: 30.8 us -> 16.7 us  [exchange(): return lax.all_to_all(x, 'mp', split_axis=0, concat_axis=0, tiled=True)]
    unnamed x39 -> x17, local copies, waits for them, and re-layouts: 14.8 us -> 3.46 us
    reduce_scatter x3 -> x2, waiting for transfers between devices: 22.8 us -> 32.3 us  [scatter_z(): lax.psum_scatter(x, 'dp', scatter_dimension=0, tiled=True, axis_index_gro...]
    all_to_all x3 -> x4, starting transfers between devices: 14.3 us -> 22 us  [exchange(): return lax.all_to_all(x, 'mp', split_axis=0, concat_axis=0, tiled=True)]
    ppermute x3, starting transfers between devices: 9.25 us -> 5.6 us  [swap_y(): return lax.ppermute(x, 'dp', [(i, i ^ 1) for i in range(Z_SIZE * Y_SIZE)])]
  transfers between devices with their start and end apart: 9 -> 12, of which waited for: 5 -> 10; matrix products, arithmetic and copies ran while one was open for 5% -> 6% of each run, Pallas kernels for 10% -> 7%
where the time goes in v2:
time: 269 us; the launch traced here: 268 us
  waiting for transfers between devices  129 us (48%)
  blocking collectives  33.7 us (13%)
  Pallas kernels  31 us (12%)
  starting transfers between devices  30.9 us (11%)
  local copies, waits for them, and re-layouts  28.9 us (11%)
  between operations  14.1 us (5%)
    ppermute x3, waiting for transfers between devices, swap_y(): return lax.ppermute(x, 'dp', [(i, i ^ 1) for i in range(Z_SIZE * Y_SIZE)])  62.5 us
    all_to_all x1, blocking collectives, exchange(): return lax.all_to_all(x, 'mp', split_axis=0, concat_axis=0, tiled=True)  33.7 us
    reduce_scatter x2, waiting for transfers between devices, scatter_z(): lax.psum_scatter(x, 'dp', scatter_dimension=0, tiled=True, axis_index_gro...  32.3 us
    all_to_all x4, starting transfers between devices, exchange(): return lax.all_to_all(x, 'mp', split_axis=0, concat_axis=0, tiled=True)  22 us
    ppermute x3, waiting for transfers between devices, shift_z(): return lax.ppermute(x, 'dp', pairs)  17.6 us
    all_to_all x4, waiting for transfers between devices, exchange(): return lax.all_to_all(x, 'mp', split_axis=0, concat_axis=0, tiled=True)  16.7 us
    slice x3, local copies, waits for them, and re-layouts, rows_of(): return array[:, :, :, first_row:first_row + rows]  15.6 us
    pallas_call x2, Pallas kernels, mix(): pl.pallas_call(body, grid_spec=pltpu.PrefetchScalarGridSpec(num_scalar_pr...  11.1 us
  transfers between devices with their start and end apart: 12, of which 10 were waited for; matrix products, arithmetic and copies ran while one was open for 6% of the time, Pallas kernels for 7%

profile of v2, /device:TPU:1, one launch (start us, length us, event | category | flops | bytes accessed | tf_op | source)
XLA Modules:
  0.0 268.2 jit_solution(10435237347970333461)
XLA Ops:
  7.2 1.9 slice.22
  9.2 7.7 %slice.18 = bf16[4,2,16,256,128]{4,3,2,1,0:T(8,128)(2,1)} slice(bf16[4,2,16,512,128]{4,3,2,1,0:T(8,128)(2,1)} %bitcast.26), slice={[0:4], [0:2], [0:16], [256:512], [0:128]} | slice | bytes 16777216 | tf_op jit(solution)/shard_map/slice | solution.py:291
  17.0 6.0 %slice.19 = bf16[4,2,16,192,128]{4,3,2,1,0:T(8,128)(2,1)} slice(bf16[4,2,16,512,128]{4,3,2,1,0:T(8,128)(2,1)} %bitcast.27), slice={[0:4], [0:2], [0:16], [0:192], [0:128]} | slice | bytes 12582912 | tf_op jit(solution)/shard_map/slice | solution.py:291
  23.0 4.5 %fusion.1 = (bf16[1,1,1,8192,128]{4,3,2,1,0:T(8,128)(2,1)}, bf16[1,1,1,8192,128]{4,3,2,1,0:T(8,128)(2,1)}) fusion(bf16[1,1,2,8192,128]{4,3,2,1,0:T(8,128)(2,1)} %param.4), kind=kLoop, calls=%fused_computation.13 | loop fusion | bytes 8388608 | tf_op jit(solution)/shard_map/slice | solution.py:304
  27.5 6.8 %all-to-all-start = ((bf16[16,512,128]{2,1,0:T(8,128)(2,1)}), bf16[16,512,128]{2,1,0:T(8,128)(2,1)}, u32[]{:S(2)}, u32[]{:S(2)}) async-start(bf16[16,512,128]{2,1,0:T(8,128)(2,1)} %bitcast.13), calls=%async_computation.2 | async-start | bytes 4194304 | tf_op jit(solution)/shard_map/all_to_all | solution.py:50
  34.4 2.6 collective-permute-start.1
  37.1 46.1 %collective-permute-done.1.received_ref = bf16[4,16,64,128]{3,2,1,0:T(8,128)(2,1)S(1)} collective-permute-done((bf16[4,16,64,128]{3,2,1,0:T(8,128)(2,1)S(1)}, bf16[4,16,64,128]{3,2,1,0:T(8,128)(2,1)S(1)}, u32[]{:S(2)}, u32[]{:S(2)}) %collective-permute-start.1) | collective-permute-done | bytes 1048608 | tf_op jit(solution)/shard_map/ppermute | solution.py:36
  83.2 2.7 %add_pair.1.refs_2_ = bf16[4,16,64,128]{3,2,1,0:T(8,128)(2,1)S(1)} custom-call(s32[2]{0:T(128)S(1)} %pad_add_fusion.1.place_ref, bf16[4,2,16,512,128]{4,3,2,1,0:T(8,128)(2,1)} %bitcast.28, bf16[4,16,64,128]{3,2,1,0:T(8,128)(2,1)S(1)} %collective-permute-done.1.received_ref), custom_call_target="tpu_custom_call" | custom-call | tf_op jit(solution)/shard_map/add_pair/pallas_call | solution.py:72
  85.9 5.4 %all-to-all-start.1 = ((bf16[16,512,128]{2,1,0:T(8,128)(2,1)}), bf16[16,512,128]{2,1,0:T(8,128)(2,1)}, u32[]{:S(2)}, u32[]{:S(2)}) async-start(bf16[16,512,128]{2,1,0:T(8,128)(2,1)} %bitcast.34), calls=%async_computation.3 | async-start | bytes 4194304 | tf_op jit(solution)/shard_map/all_to_all | solution.py:50
  91.3 9.8 %reduce-scatter.5.cloned.1.call-done = bf16[32,256,128]{2,1,0:T(8,128)(2,1)} async-done(((bf16[128,256,128]{2,1,0:T(8,128)(2,1)}), bf16[32,256,128]{2,1,0:T(8,128)(2,1)}) %reduce-scatter.5.cloned.1.call-update) | async-done | bytes 2097168 | tf_op jit(solution)/shard_map/reduce_scatter | solution.py:40
  101.1 2.3 dynamic-slice_bitcast_fusion
  103.4 2.7 %collective-permute-start = (bf16[16,256,128]{2,1,0:T(8,128)(2,1)}, bf16[16,256,128]{2,1,0:T(8,128)(2,1)S(1)}, u32[]{:S(2)}, u32[]{:S(2)}) collective-permute-start(bf16[16,256,128]{2,1,0:T(8,128)(2,1)} %dynamic-slice_bitcast_fusion), channel_id=1, source_target_pairs={{0,16},{16,0},{32,48},{48,32},{64,80},{80,64},{96,112},{112,96},{1... | collective-permute-start | bytes 3145736 | tf_op jit(solution)/shard_map/ppermute | solution.py:36
  106.9 1.7 collective-permute-start.3
  108.6 1.6 collective-permute-start.4
  110.6 6.1 %collective-permute-done.2.refs_3_ = bf16[16,64,128]{2,1,0:T(8,128)(2,1)S(1)} collective-permute-done((bf16[16,64,128]{2,1,0:T(8,128)(2,1)}, bf16[16,64,128]{2,1,0:T(8,128)(2,1)S(1)}, u32[]{:S(2)}, u32[]{:S(2)}) %collective-permute-start.2) | collective-permute-done | bytes 262176 | tf_op jit(solution)/shard_map/ppermute | solution.py:57
  116.6 7.5 %collective-permute-done.3.refs_4_ = bf16[16,64,128]{2,1,0:T(8,128)(2,1)S(1)} collective-permute-done((bf16[16,64,128]{2,1,0:T(8,128)(2,1)S(1)}, bf16[16,64,128]{2,1,0:T(8,128)(2,1)S(1)}, u32[]{:S(2)}, u32[]{:S(2)}) %collective-permute-start.3) | collective-permute-done | bytes 262176 | tf_op jit(solution)/shard_map/ppermute | solution.py:57
  124.1 4.1 %collective-permute-done.4.refs_5_ = bf16[16,64,128]{2,1,0:T(8,128)(2,1)S(1)} collective-permute-done((bf16[16,64,128]{2,1,0:T(8,128)(2,1)S(1)}, bf16[16,64,128]{2,1,0:T(8,128)(2,1)S(1)}, u32[]{:S(2)}, u32[]{:S(2)}) %collective-permute-start.4) | collective-permute-done | bytes 262176 | tf_op jit(solution)/shard_map/ppermute | solution.py:57
  128.2 10.8 %collective-permute-done.refs_1_ = bf16[16,256,128]{2,1,0:T(8,128)(2,1)S(1)} collective-permute-done((bf16[16,256,128]{2,1,0:T(8,128)(2,1)}, bf16[16,256,128]{2,1,0:T(8,128)(2,1)S(1)}, u32[]{:S(2)}, u32[]{:S(2)}) %collective-permute-start) | collective-permute-done | bytes 1048608 | tf_op jit(solution)/shard_map/ppermute | solution.py:36
  139.0 6.0 %mix.2 = (bf16[16,640,128]{2,1,0:T(8,128)(2,1)}, bf16[16,320,128]{2,1,0:T(8,128)(2,1)S(1)}, f32[16,128,128]{2,1,0:T(8,128)S(1)}) custom-call(s32[18]{0:T(128)S(1)} %pad_add_fusion.index_ref, bf16[2,16,256,128]{3,2,1,0:T(8,128)(2,1)} %bitcast.36, bf16[16,256,128]{2,1,0:T(8,128)(2,1)S(1)} %collective-permute-done.refs_1_, ...), custom_call_target="tpu_custom_call" | custom-call | tf_op jit(solution)/shard_map/mix/pallas_call | solution.py:157
  147.1 5.3 %all-to-all-start.2 = ((bf16[16,640,128]{2,1,0:T(8,128)(2,1)}), bf16[16,640,128]{2,1,0:T(8,128)(2,1)S(1)}, u32[]{:S(2)}, u32[]{:S(2)}) async-start(bf16[16,640,128]{2,1,0:T(8,128)(2,1)} %get-tuple-element.26), calls=%async_computation.4 | async-start | bytes 5242880 | tf_op jit(solution)/shard_map/all_to_all | solution.py:50
  152.4 22.5 %reduce-scatter.3.cloned.1.call-done = bf16[32,192,128]{2,1,0:T(8,128)(2,1)} async-done(((bf16[128,192,128]{2,1,0:T(8,128)(2,1)}), bf16[32,192,128]{2,1,0:T(8,128)(2,1)}) %reduce-scatter.3.cloned.1.call-update) | async-done | bytes 1572880 | tf_op jit(solution)/shard_map/reduce_scatter | solution.py:40
  174.9 2.1 dynamic-slice_bitcast_fusion.2
  177.4 9.9 %all-to-all-done.2.arrived_ref = bf16[16,640,128]{2,1,0:T(8,128)(2,1)S(1)} async-done(((bf16[16,640,128]{2,1,0:T(8,128)(2,1)}), bf16[16,640,128]{2,1,0:T(8,128)(2,1)S(1)}, u32[]{:S(2)}, u32[]{:S(2)}) %all-to-all-start.2) | async-done | bytes 2621472 | tf_op jit(solution)/shard_map/all_to_all | solution.py:50
  187.3 7.9 %renew.2.refs_0_ = bf16[2,16,512,128]{3,2,1,0:T(8,128)(2,1)} custom-call(s32[2]{0:T(128)S(1)} %fusion.filled_ref, bf16[2,16,512,128]{3,2,1,0:T(8,128)(2,1)} %bitcast.29, bf16[16,640,128]{2,1,0:T(8,128)(2,1)S(1)} %all-to-all-done.2.arrived_ref), custom_call_target="tpu_custom_call" | custom-call | tf_op jit(solution)/shard_map/renew/pallas_call | solution.py:251
  195.2 5.5 %collective-permute-done.5.refs_1_ = bf16[16,192,128]{2,1,0:T(8,128)(2,1)S(1)} collective-permute-done((bf16[16,192,128]{2,1,0:T(8,128)(2,1)}, bf16[16,192,128]{2,1,0:T(8,128)(2,1)S(1)}, u32[]{:S(2)}, u32[]{:S(2)}) %collective-permute-start.5) | collective-permute-done | bytes 786464 | tf_op jit(solution)/shard_map/ppermute | solution.py:36
  200.8 5.1 %mix.3 = (bf16[16,512,128]{2,1,0:T(8,128)(2,1)}, bf16[16,192,128]{2,1,0:T(8,128)(2,1)S(1)}) custom-call(s32[18]{0:T(128)S(1)} %pad_add_fusion.index_ref, bf16[2,16,192,128]{3,2,1,0:T(8,128)(2,1)S(1)} %bitcast.24, bf16[16,192,128]{2,1,0:T(8,128)(2,1)S(1)} %collective-permute-done.5.refs_1_, bf16[16,512,128]{2,1,0:T(8,128)(2,1)} %all-to-all-done.refs_6_.refs_2_, ...), custom_call_target="tpu_custom_call" | custom-call | tf_op jit(solution)/shard_map/mix/pallas_call | solution.py:157
  205.9 33.7 %all_to_all.25.parts_ref.arrived_ref = bf16[16,512,128]{2,1,0:T(8,128)(2,1)S(1)} all-to-all(bf16[16,512,128]{2,1,0:T(8,128)(2,1)} %get-tuple-element.32), channel_id=1, replica_groups=mesh['dp'=8,'mp'=16] {'mp'}, dimensions={0} | all-to-all | bytes 4194304 | tf_op jit(solution)/shard_map/all_to_all | solution.py:50
  239.5 2.1 polynomial.1
  241.7 4.4 %all-to-all-start.4 = ((bf16[16,128,128]{2,1,0:T(8,128)(2,1)}), bf16[16,128,128]{2,1,0:T(8,128)(2,1)S(1)}, u32[]{:S(2)}, u32[]{:S(2)}) async-start(bf16[16,128,128]{2,1,0:T(8,128)(2,1)} %polynomial.1), calls=%async_computation.6 | async-start | bytes 1048576 | tf_op jit(solution)/shard_map/all_to_all | solution.py:50
  246.1 3.2 %renew.3 = bf16[2,16,512,128]{3,2,1,0:T(8,128)(2,1)} custom-call(s32[2]{0:T(128)S(1)} %fusion.filled_ref, bf16[2,16,512,128]{3,2,1,0:T(8,128)(2,1)} %bitcast.30, bf16[16,512,128]{2,1,0:T(8,128)(2,1)S(1)} %all_to_all.25.parts_ref.arrived_ref, bf16[2,16,512,128]{3,2,1,0:T(8,128)(2,1)} %renew.2.refs_0_), custom_call_target="tpu_custom_call", output_to_operand_aliasing={{}: (3, {})} | custom-call | tf_op jit(solution)/shard_map/renew/pallas_call | solution.py:251
  249.3 6.8 %all-to-all-done.4.turn_ref = bf16[16,128,128]{2,1,0:T(8,128)(2,1)S(1)} async-done(((bf16[16,128,128]{2,1,0:T(8,128)(2,1)}), bf16[16,128,128]{2,1,0:T(8,128)(2,1)S(1)}, u32[]{:S(2)}, u32[]{:S(2)}) %all-to-all-start.4) | async-done | bytes 524320 | tf_op jit(solution)/shard_map/all_to_all | solution.py:50
  257.4 3.9 %turn_all.1 = bf16[16,512,128]{2,1,0:T(8,128)(2,1)} custom-call(bf16[16,192,128]{2,1,0:T(8,128)(2,1)S(1)} %copy-done.6, bf16[16,320,128]{2,1,0:T(8,128)(2,1)S(1)} %copy-done.2, bf16[16,128,128]{2,1,0:T(8,128)(2,1)S(1)} %all-to-all-done.4.turn_ref), custom_call_target="tpu_custom_call" | custom-call | tf_op jit(solution)/shard_map/turn_all/pallas_call | solution.py:222
  (32 shorter events, 5.2 us)
Async XLA Ops:
  7.2 94.0 %reduce-scatter.5.cloned.1.call-start = ((), (), s32[]{:S(2)}) async-start(), calls=%async_computation.8 | async-start | bytes 10485760 | tf_op jit(solution)/shard_map/reduce_scatter | solution.py:40
  17.0 157.9 %reduce-scatter.3.cloned.1.call-start = ((), (), s32[]{:S(2)}) async-start(), calls=%async_computation.7 | async-start | bytes 7864320 | tf_op jit(solution)/shard_map/reduce_scatter | solution.py:40
  27.5 58.4 %all-to-all-start = ((bf16[16,512,128]{2,1,0:T(8,128)(2,1)}), bf16[16,512,128]{2,1,0:T(8,128)(2,1)}, u32[]{:S(2)}, u32[]{:S(2)}) async-start(bf16[16,512,128]{2,1,0:T(8,128)(2,1)} %bitcast.13), calls=%async_computation.2 | async-start | bytes 4194304 | tf_op jit(solution)/shard_map/all_to_all | solution.py:50
  34.4 48.8 %collective-permute-start.1 = (bf16[4,16,64,128]{3,2,1,0:T(8,128)(2,1)S(1)}, bf16[4,16,64,128]{3,2,1,0:T(8,128)(2,1)S(1)}, u32[]{:S(2)}, u32[]{:S(2)}) collective-permute-start(bf16[4,16,64,128]{3,2,1,0:T(8,128)(2,1)S(1)} %dynamic-slice_bitcast_fusion.1), channel_id=1, source_target_pairs={{0,16},{16,0},{32,48},{48,32},{64,80},{80,64},{96,112},{112,96},{1... | collective-permute-start | bytes 3145736 | tf_op jit(solution)/shard_map/ppermute | solution.py:36
  85.9 42.3 %all-to-all-start.1 = ((bf16[16,512,128]{2,1,0:T(8,128)(2,1)}), bf16[16,512,128]{2,1,0:T(8,128)(2,1)}, u32[]{:S(2)}, u32[]{:S(2)}) async-start(bf16[16,512,128]{2,1,0:T(8,128)(2,1)} %bitcast.34), calls=%async_computation.3 | async-start | bytes 4194304 | tf_op jit(solution)/shard_map/all_to_all | solution.py:50
  91.3 18.9 %copy-start.7 = (s32[1,16,2]{1,2,0:T(2,128)S(1)}, s32[1,16,2]{1,2,0:T(2,128)}, u32[]{:S(2)}) copy-start(s32[1,16,2]{1,2,0:T(2,128)} %param.5) | copy-start | bytes 388
  103.4 35.6 %collective-permute-start = (bf16[16,256,128]{2,1,0:T(8,128)(2,1)}, bf16[16,256,128]{2,1,0:T(8,128)(2,1)S(1)}, u32[]{:S(2)}, u32[]{:S(2)}) collective-permute-start(bf16[16,256,128]{2,1,0:T(8,128)(2,1)} %dynamic-slice_bitcast_fusion), channel_id=1, source_target_pairs={{0,16},{16,0},{32,48},{48,32},{64,80},{80,64},{96,112},{112,96},{1... | collective-permute-start | bytes 3145736 | tf_op jit(solution)/shard_map/ppermute | solution.py:36
  106.9 9.7 %collective-permute-start.2 = (bf16[16,64,128]{2,1,0:T(8,128)(2,1)}, bf16[16,64,128]{2,1,0:T(8,128)(2,1)S(1)}, u32[]{:S(2)}, u32[]{:S(2)}) collective-permute-start(bf16[16,64,128]{2,1,0:T(8,128)(2,1)} %get-tuple-element.38), channel_id=1, source_target_pairs={{0,32},{16,48},{32,64},{48,80},{64,96},{80,112},{96,0},{112,16},{1... | collective-permute-start | bytes 786440 | tf_op jit(solution)/shard_map/ppermute | solution.py:57
  106.9 17.2 %collective-permute-start.3 = (bf16[16,64,128]{2,1,0:T(8,128)(2,1)S(1)}, bf16[16,64,128]{2,1,0:T(8,128)(2,1)S(1)}, u32[]{:S(2)}, u32[]{:S(2)}) collective-permute-start(bf16[16,64,128]{2,1,0:T(8,128)(2,1)S(1)} %get-tuple-element.37), channel_id=1, source_target_pairs={{0,64},{16,80},{32,96},{48,112},{64,0},{80,16},{96,32},{112,48},{1... | collective-permute-start | bytes 786440 | tf_op jit(solution)/shard_map/ppermute | solution.py:57
  108.6 19.6 %collective-permute-start.4 = (bf16[16,64,128]{2,1,0:T(8,128)(2,1)S(1)}, bf16[16,64,128]{2,1,0:T(8,128)(2,1)S(1)}, u32[]{:S(2)}, u32[]{:S(2)}) collective-permute-start(bf16[16,64,128]{2,1,0:T(8,128)(2,1)S(1)} %get-tuple-element.36), channel_id=1, source_target_pairs={{0,96},{16,112},{32,0},{48,16},{64,32},{80,48},{96,64},{112,80},{1... | collective-permute-start | bytes 786440 | tf_op jit(solution)/shard_map/ppermute | solution.py:57
  145.0 1.1 copy-start.1
  146.1 1.0 copy-start.3
  147.1 40.2 %all-to-all-start.2 = ((bf16[16,640,128]{2,1,0:T(8,128)(2,1)}), bf16[16,640,128]{2,1,0:T(8,128)(2,1)S(1)}, u32[]{:S(2)}, u32[]{:S(2)}) async-start(bf16[16,640,128]{2,1,0:T(8,128)(2,1)} %get-tuple-element.26), calls=%async_computation.4 | async-start | bytes 5242880 | tf_op jit(solution)/shard_map/all_to_all | solution.py:50
  177.0 23.8 %collective-permute-start.5 = (bf16[16,192,128]{2,1,0:T(8,128)(2,1)}, bf16[16,192,128]{2,1,0:T(8,128)(2,1)S(1)}, u32[]{:S(2)}, u32[]{:S(2)}) collective-permute-start(bf16[16,192,128]{2,1,0:T(8,128)(2,1)} %dynamic-slice_bitcast_fusion.2), channel_id=1, source_target_pairs={{0,16},{16,0},{32,48},{48,32},{64,80},{80,64},{96,112},{112,96},{1... | collective-permute-start | bytes 2359304 | tf_op jit(solution)/shard_map/ppermute | solution.py:36
  187.3 13.5 %copy-start = (bf16[32,192,128]{2,1,0:T(8,128)(2,1)S(1)}, bf16[32,192,128]{2,1,0:T(8,128)(2,1)}, u32[]{:S(2)}) copy-start(bf16[32,192,128]{2,1,0:T(8,128)(2,1)} %reduce-scatter.3.cloned.1.call-done) | copy-start | bytes 4718596
  187.3 13.5 %copy-start.4 = (f32[16,128,128]{2,1,0:T(8,128)S(1)}, f32[16,128,128]{2,1,0:T(8,128)}, u32[]{:S(2)}) copy-start(f32[16,128,128]{2,1,0:T(8,128)} %copy-done.3) | copy-start | bytes 3145732
  205.9 33.7 %copy-start.5 = (bf16[16,192,128]{2,1,0:T(8,128)(2,1)}, bf16[16,192,128]{2,1,0:T(8,128)(2,1)S(1)}, u32[]{:S(2)}) copy-start(bf16[16,192,128]{2,1,0:T(8,128)(2,1)S(1)} %get-tuple-element.30.late_ref) | copy-start | bytes 2359300
  241.7 14.4 %all-to-all-start.4 = ((bf16[16,128,128]{2,1,0:T(8,128)(2,1)}), bf16[16,128,128]{2,1,0:T(8,128)(2,1)S(1)}, u32[]{:S(2)}, u32[]{:S(2)}) async-start(bf16[16,128,128]{2,1,0:T(8,128)(2,1)} %polynomial.1), calls=%async_computation.6 | async-start | bytes 1048576 | tf_op jit(solution)/shard_map/all_to_all | solution.py:50
  246.1 10.0 %copy-start.6 = (bf16[16,192,128]{2,1,0:T(8,128)(2,1)S(1)}, bf16[16,192,128]{2,1,0:T(8,128)(2,1)}, u32[]{:S(2)}) copy-start(bf16[16,192,128]{2,1,0:T(8,128)(2,1)} %copy-done.5) | copy-start | bytes 2359300
  256.1 1.3 copy-start.2
Sparse Core Ops, SparseCore 0:
  17.1 83.9 reduce-scatter.4
  103.5 71.3 reduce-scatter.2

commit v3 on v2

--- a/solution.py
+++ b/solution.py
@@ -19,8 +19,8 @@
 
 Z_SIZE = 4
 Y_SIZE = 2
-EARLY, PAIRED, LATE = (256, 256), (192, 64), (0, 192)
-SOON = (192, 320)
+PAIRED, LATE, EARLY = (0, 64), (64, 176), (240, 272)
+LAST = (0, 240)
 VMEM = 48 * 1024 * 1024
 
 
@@ -59,6 +59,34 @@
 
 def whole(*shape):
     return pl.BlockSpec(shape, lambda n, i: (0,) * len(shape))
+
+
+def copy_rows(place, own, chunk, blocks, steps, at):
+    first_row, rows = chunk
+    mats = own.shape[2]
+
+    def body(place_ref, *refs):
+        for source, target in zip(refs[:blocks], refs[blocks:]):
+            target[...] = source[0]
+
+    return pl.pallas_call(
+        body,
+        grid_spec=pltpu.PrefetchScalarGridSpec(
+            num_scalar_prefetch=1,
+            grid=(steps,),
+            in_specs=[
+                pl.BlockSpec(
+                    (1, 1, mats, rows, HEAD),
+                    lambda n, i, block=block: (*at(block, n, i), 0, first_row // rows, 0),
+                )
+                for block in range(blocks)
+            ],
+            out_specs=[pl.BlockSpec((1, mats, rows, HEAD), lambda n, i: (n, 0, 0, 0))] * blocks,
+        ),
+        out_shape=[jax.ShapeDtypeStruct((steps, mats, rows, HEAD), jnp.bfloat16)] * blocks,
+        compiler_params=params(),
+        name="copy_rows",
+    )(place, *[own] * blocks)
 
 
 def add_pair(place, own, received, first_row, rows):
@@ -90,7 +118,7 @@
 
 def mix(index, pieces, held, gram, last):
     mats = index.shape[0] - 2
-    owners, piece = held[0].shape[:2]
+    owners = held.shape[0]
     begun = gram is not None
     total = sum(rows for _, rows, _ in pieces)
     base = min(first_row for first_row, _, _ in pieces)
@@ -100,25 +128,24 @@
     def body(index_ref, *refs):
         refs = list(refs)
         term_refs = [refs.pop(0) for _ in terms]
-        held_refs = [refs.pop(0) for _ in held]
+        held_ref = refs.pop(0)
         before_ref = refs.pop(0) if begun else None
         sent_ref, mixed_ref = refs[:2]
         for k in range(mats):
             owner, slot = index_ref[2 + k] // 2, index_ref[2 + k] % 2
             part = before_ref[k] if begun else None
-            unread = list(zip(term_refs, terms))
+            unread = list(term_refs)
             for first_row, rows, group in pieces:
                 here, unread = unread[: len(group)], unread[len(group) :]
                 summed = sum(
-                    (ref[0, k] if isinstance(term, tuple) else ref[k]).astype(jnp.float32)
-                    for ref, term in here
+                    ref[(0,) * (len(ref.shape) - 3) + (k,)].astype(jnp.float32)
+                    for ref in here
                 )
                 rounded = summed.astype(jnp.bfloat16)
                 start = pl.multiple_of(lead + first_row - base + slot * total, 16)
                 sent_ref[owner, pl.ds(start, rows)] = rounded
                 summed = rounded.astype(jnp.float32)
-                first, second = (ref[owner, first_row : first_row + rows] for ref in held_refs)
-                stored = jnp.where(slot == 1, second.astype(jnp.float32), first.astype(jnp.float32))
+                stored = held_ref[owner, slot, first_row : first_row + rows].astype(jnp.float32)
                 renewed = (momentum_rate * stored + summed).astype(jnp.bfloat16)
                 mixed = (summed + momentum_rate * renewed.astype(jnp.float32)).astype(jnp.bfloat16)
                 mixed_ref[k, first_row - base : first_row - base + rows] = mixed
@@ -136,15 +163,14 @@
         for term in group:
             if isinstance(term, tuple):
                 in_specs.append(
-                    pl.BlockSpec((1, mats, rows, HEAD), lambda n, i, at=term[1]: (i[at], 0, 0, 0))
+                    pl.BlockSpec((1,) * (term[0].ndim - 3) + (mats, rows, HEAD), term[1])
                 )
                 operands.append(term[0])
             else:
                 in_specs.append(whole(mats, rows, HEAD))
                 operands.append(term)
-    for one in held:
-        in_specs.append(whole(owners, piece, HEAD))
-        operands.append(one)
+    in_specs.append(whole(*held.shape))
+    operands.append(held)
     if begun:
         in_specs.append(whole(mats, HEAD, HEAD))
         operands.append(gram)
@@ -204,14 +230,14 @@
     )(parts)
 
 
-def turn_all(late, soon, turns):
+def turn_all(last, early, turns):
     mats = turns.shape[0]
-    piece = LATE[1] + SOON[1]
+    piece = LAST[1] + EARLY[1]
     per = 2
 
-    def body(late_ref, soon_ref, turn_ref, out_ref):
+    def body(last_ref, early_ref, turn_ref, out_ref):
         for k in range(per):
-            for ref, (first_row, rows) in ((late_ref, LATE), (soon_ref, SOON)):
+            for ref, (first_row, rows) in ((last_ref, LAST), (early_ref, EARLY)):
                 out_ref[k, first_row : first_row + rows] = jnp.dot(
                     ref[k], turn_ref[k], preferred_element_type=jnp.float32
                 ).astype(jnp.bfloat16)
@@ -222,40 +248,41 @@
     return pl.pallas_call(
         body,
         grid=(mats // per,),
-        in_specs=[block(LATE[1]), block(SOON[1]), block(HEAD)],
+        in_specs=[block(LAST[1]), block(EARLY[1]), block(HEAD)],
         out_specs=block(piece),
         out_shape=jax.ShapeDtypeStruct((mats, piece, HEAD), jnp.bfloat16),
         compiler_params=params(),
         name="turn_all",
-    )(late, soon, turns)
+    )(last, early, turns)
 
 
 def renew(filled, stored, arrived, done, first_row, rows):
     slots, sources, _, _ = stored.shape
     lead = arrived.shape[1] - slots * rows
-    unit = math.gcd(first_row, rows)
-    per = 8
+    piece = rows if first_row % rows == 0 else stored.shape[2]
+    at = 0 if first_row % rows == 0 else first_row
+    per = 4
 
     def body(filled_ref, stored_ref, arrived_ref, *refs):
         out_ref = refs[-1]
-        at = pl.program_id(1) * unit
+        here = slice(at, at + rows)
         for slot in range(slots):
-            start = pl.multiple_of(lead + slot * rows + at, 16)
-            grad = arrived_ref[:, pl.ds(start, unit)].astype(jnp.float32)
+            start = lead + slot * rows
+            grad = arrived_ref[:, start : start + rows].astype(jnp.float32)
             grad = jnp.where(filled_ref[slot] == 1, grad, 0.0)
-            out_ref[slot] = (
-                momentum_rate * stored_ref[slot].astype(jnp.float32) + grad
+            out_ref[slot, :, here] = (
+                momentum_rate * stored_ref[slot, :, here].astype(jnp.float32) + grad
             ).astype(jnp.bfloat16)
 
-    here = pl.BlockSpec((slots, per, unit, HEAD), lambda p, r, f: (0, p, first_row // unit + r, 0))
+    block = pl.BlockSpec((slots, per, piece, HEAD), lambda p, f: (0, p, first_row // piece, 0))
     return pl.pallas_call(
         body,
         grid_spec=pltpu.PrefetchScalarGridSpec(
             num_scalar_prefetch=1,
-            grid=(sources // per, rows // unit),
-            in_specs=[here, pl.BlockSpec((per, lead + slots * rows, HEAD), lambda p, r, f: (p, 0, 0))]
+            grid=(sources // per,),
+            in_specs=[block, pl.BlockSpec((per, lead + slots * rows, HEAD), lambda p, f: (p, 0, 0))]
             + [pl.BlockSpec(memory_space=pl.ANY)] * (done is not None),
-            out_specs=here,
+            out_specs=block,
         ),
         out_shape=jax.ShapeDtypeStruct(stored.shape, jnp.bfloat16),
         input_output_aliases={3: 0} if done is not None else {},
@@ -286,44 +313,45 @@
     def half_away(part):
         return lax.dynamic_index_in_dim(part, 1 - half, 0, keepdims=False)
 
-    def rows_of(array, chunk):
-        first_row, rows = chunk
-        return array[:, :, :, first_row : first_row + rows]
-
-    away, own1 = barrier(
-        lax.dynamic_index_in_dim(rows_of(own, PAIRED), 1 - half, 1, keepdims=False), own
-    )
-    early, own2 = barrier(rows_of(own1, EARLY), own1)
-    late = rows_of(own2, LATE)
-    early, late = (
-        scatter_z(part.reshape(-1, part.shape[3], HEAD)).reshape(Y_SIZE, mats, -1, HEAD)
-        for part in (early, late)
-    )
-    received, later = barrier(swap_y(away), stored[1])
-    paired, later = barrier(add_pair(place, own, received, *PAIRED), later)
-    held = [exchange(stored[0]), exchange(later)]
+    def own_half(n, i):
+        return (i[0], 0, 0, 0)
+
+    def own_level(n, i):
+        return (i[1], 0, 0, 0)
+
+    def half_away(part):
+        return lax.dynamic_index_in_dim(part, 1 - half, 0, keepdims=False)
+
+    early, own1 = barrier(own[:, :, :, EARLY[0] : EARLY[0] + EARLY[1]], own)
+    early = scatter_z(early.reshape(-1, EARLY[1], HEAD)).reshape(Y_SIZE, mats, -1, HEAD)
+    (away,) = copy_rows(place, own1, PAIRED, 1, Z_SIZE, lambda block, n, i: (n, 1 - i[0]))
+    away, turned = barrier(away, stored.swapaxes(0, 1))
+    turned, own2 = barrier(turned, own1)
+    received = swap_y(away)
+    held, own2 = barrier(exchange(turned), own2)
+    late = own2[:, :, :, LATE[0] : LATE[0] + LATE[1]].reshape(-1, LATE[1], HEAD)
+    late = scatter_z(late).reshape(Y_SIZE, mats, -1, HEAD)
+    early, held, received = barrier(early, held, received)
+    early_away = swap_y(half_away(early))
+    paired = add_pair(place, own, received, *PAIRED)
     shifted = [
         shift_z(lax.dynamic_index_in_dim(paired, (level + by) % Z_SIZE, 0, keepdims=False), by)
         for by in range(1, Z_SIZE)
     ]
-    sent, mixed_soon, gram = mix(
-        index,
-        [
-            (*EARLY, [(early, 0), swap_y(half_away(early))]),
-            (*PAIRED, [(paired, 1), *shifted]),
-        ],
-        held,
-        None,
-        False,
-    )
+    pieces = [(*EARLY, [(early, own_half), early_away])]
+    sent, mixed_early, gram = mix(index, pieces, held, None, False)
     late, _ = barrier(late, sent)
-    renewed = renew(filled, stored, exchange(sent), None, *SOON)
+    renewed = renew(filled, stored, exchange(sent), None, *EARLY)
     renewed, received = barrier(renewed, swap_y(half_away(late)))
-    sent, mixed_late = mix(index, [(*LATE, [(late, 0), received])], held, gram, True)
+    pieces = [
+        (*PAIRED, [(paired, own_level), *shifted]),
+        (*LATE, [(late, own_half), received]),
+    ]
+    sent, mixed_last = mix(index, pieces, held, gram, True)
     arrived = exchange(sent)
     turns = exchange(polynomial(arrived))
-    renewed = renew(filled, stored, arrived, renewed, *LATE)
-    update = turn_all(mixed_late, mixed_soon, turns)
+    renewed = renew(filled, stored, arrived, renewed, *LAST)
+    update = turn_all(mixed_last, mixed_early, turns)
     return (update, renewed.reshape(1, 1, slots, -1, HEAD))
 
 

time: 269 us -> 265 us (0.985)
  blocking collectives: 33.7 us -> 92.4 us
  waiting for transfers between devices: 129 us -> 75 us
  starting transfers between devices: 30.9 us -> 23.5 us
  local copies, waits for them, and re-layouts: 28.9 us -> 26.2 us
    all_to_all x1 -> x2, blocking collectives: 33.7 us -> 92.4 us  [exchange(): return lax.all_to_all(x, 'mp', split_axis=0, concat_axis=0, tiled=True)]
    ppermute x3, waiting for transfers between devices: 17.6 us -> 0.01 us  [shift_z(): return lax.ppermute(x, 'dp', pairs)]
    reduce_scatter x2, waiting for transfers between devices: 32.3 us -> 16.7 us  [scatter_z(): lax.psum_scatter(x, 'dp', scatter_dimension=0, tiled=True, axis_index_gro...]
    all_to_all x4 -> x2, waiting for transfers between devices: 16.7 us -> 5.42 us  [exchange(): return lax.all_to_all(x, 'mp', split_axis=0, concat_axis=0, tiled=True)]
    all_to_all x4 -> x2, starting transfers between devices: 22 us -> 12.1 us  [exchange(): return lax.all_to_all(x, 'mp', split_axis=0, concat_axis=0, tiled=True)]
    ppermute x3, waiting for transfers between devices: 62.5 us -> 52.8 us  [swap_y(): return lax.ppermute(x, 'dp', [(i, i ^ 1) for i in range(Z_SIZE * Y_SIZE)])]
    slice x4 -> x2, local copies, waits for them, and re-layouts: 20.1 us -> 13.3 us  [the longest x1 7.65 us: on_device(): early, own1 = barrier(own[:, :, :, EARLY[0]:EARLY[0] + EARLY[1]], own)]
    unnamed x17 -> x25, local copies, waits for them, and re-layouts: 3.46 us -> 8.08 us
  transfers between devices with their start and end apart: 12 -> 10, of which waited for: 10 -> 5; matrix products, arithmetic and copies ran while one was open for 6% -> 4% of each run, Pallas kernels for 7% -> 8%
where the time goes in v3:
time: 265 us; the launch traced here: 264 us
  blocking collectives  92.4 us (35%)
  waiting for transfers between devices  75 us (28%)
  Pallas kernels  32.4 us (12%)
  local copies, waits for them, and re-layouts  26.2 us (10%)
  starting transfers between devices  23.5 us (9%)
  between operations  14.2 us (5%)
    all_to_all x2, blocking collectives, exchange(): return lax.all_to_all(x, 'mp', split_axis=0, concat_axis=0, tiled=True)  92.4 us
    ppermute x3, waiting for transfers between devices, swap_y(): return lax.ppermute(x, 'dp', [(i, i ^ 1) for i in range(Z_SIZE * Y_SIZE)])  52.8 us
    reduce_scatter x2, waiting for transfers between devices, scatter_z(): lax.psum_scatter(x, 'dp', scatter_dimension=0, tiled=True, axis_index_gro...  16.7 us
    all_to_all x2, starting transfers between devices, exchange(): return lax.all_to_all(x, 'mp', split_axis=0, concat_axis=0, tiled=True)  12.1 us
    pallas_call x2, Pallas kernels, renew(): pl.pallas_call(body, grid_spec=pltpu.PrefetchScalarGridSpec(num_scalar_pr...  10.3 us
    pallas_call x2, Pallas kernels, mix(): pl.pallas_call(body, grid_spec=pltpu.PrefetchScalarGridSpec(num_scalar_pr...  10.1 us
    ppermute x3, starting transfers between devices, swap_y(): return lax.ppermute(x, 'dp', [(i, i ^ 1) for i in range(Z_SIZE * Y_SIZE)])  8.11 us
    unnamed x25, local copies, waits for them, and re-layouts  8.08 us
  transfers between devices with their start and end apart: 10, of which 5 were waited for; matrix products, arithmetic and copies ran while one was open for 4% of the time, Pallas kernels for 8%

profile of v3, /device:TPU:1, one launch (start us, length us, event | category | flops | bytes accessed | tf_op | source)
XLA Modules:
  0.0 264.1 jit_solution(16217815581541185691)
XLA Ops:
  7.2 7.7 %slice.8 = bf16[4,2,16,272,128]{4,3,2,1,0:T(8,128)(2,1)} slice(bf16[4,2,16,512,128]{4,3,2,1,0:T(8,128)(2,1)} %bitcast.23), slice={[0:4], [0:2], [0:16], [240:512], [0:128]} | slice | bytes 17825792 | tf_op jit(solution)/shard_map/slice | solution.py:325
  15.0 2.9 %copy_rows.1 = bf16[4,16,64,128]{3,2,1,0:T(8,128)(2,1)S(1)} custom-call(s32[2]{0:T(128)S(1)} %pad_add_fusion.1.place_ref, bf16[4,2,16,512,128]{4,3,2,1,0:T(8,128)(2,1)} %bitcast.24), custom_call_target="tpu_custom_call" | custom-call | tf_op jit(solution)/shard_map/copy_rows/pallas_call | solution.py:72
  18.4 55.9 %all_to_all.20.refs_2_.refs_6_ = bf16[16,2,512,128]{3,2,1,0:T(8,128)(2,1)} all-to-all(bf16[16,2,512,128]{3,2,1,0:T(8,128)(2,1)S(1)} %copy.15), channel_id=1, replica_groups=mesh['dp'=8,'mp'=16] {'mp'}, dimensions={0} | all-to-all | bytes 8388608 | tf_op jit(solution)/shard_map/all_to_all | solution.py:50
  74.3 5.7 %slice.7 = bf16[4,2,16,176,128]{4,3,2,1,0:T(8,128)(2,1)} slice(bf16[4,2,16,512,128]{4,3,2,1,0:T(8,128)(2,1)} %bitcast.25), slice={[0:4], [0:2], [0:16], [64:240], [0:128]} | slice | bytes 11534336 | tf_op jit(solution)/shard_map/slice | solution.py:332
  80.0 2.7 %collective-permute-start = (bf16[4,16,64,128]{3,2,1,0:T(8,128)(2,1)S(1)}, bf16[4,16,64,128]{3,2,1,0:T(8,128)(2,1)S(1)}, u32[]{:S(2)}, u32[]{:S(2)}) collective-permute-start(bf16[4,16,64,128]{3,2,1,0:T(8,128)(2,1)S(1)} %copy_rows.1), channel_id=1, source_target_pairs={{0,16},{16,0},{32,48},{48,32},{64,80},{80,64},{96,112},{112,96},{1... | collective-permute-start | bytes 3145736 | tf_op jit(solution)/shard_map/ppermute | solution.py:36
  82.7 22.5 %collective-permute-done.received_ref = bf16[4,16,64,128]{3,2,1,0:T(8,128)(2,1)S(1)} collective-permute-done((bf16[4,16,64,128]{3,2,1,0:T(8,128)(2,1)S(1)}, bf16[4,16,64,128]{3,2,1,0:T(8,128)(2,1)S(1)}, u32[]{:S(2)}, u32[]{:S(2)}) %collective-permute-start) | collective-permute-done | bytes 1048608 | tf_op jit(solution)/shard_map/ppermute | solution.py:36
  105.2 1.0 copy-done.6
  106.2 1.3 dynamic-slice_bitcast_fusion
  107.5 2.7 %collective-permute-start.4 = (bf16[16,272,128]{2,1,0:T(8,128)(2,1)S(1)}, bf16[16,272,128]{2,1,0:T(8,128)(2,1)S(1)}, u32[]{:S(2)}, u32[]{:S(2)}) collective-permute-start(bf16[16,272,128]{2,1,0:T(8,128)(2,1)S(1)} %dynamic-slice_bitcast_fusion), channel_id=1, source_target_pairs={{0,16},{16,0},{32,48},{48,32},{64,80},{80,64},{96,112},{112,96},{1... | collective-permute-start | bytes 3342344 | tf_op jit(solution)/shard_map/ppermute | solution.py:36
  110.6 22.6 %collective-permute-done.4.refs_1_ = bf16[16,272,128]{2,1,0:T(8,128)(2,1)S(1)} collective-permute-done((bf16[16,272,128]{2,1,0:T(8,128)(2,1)S(1)}, bf16[16,272,128]{2,1,0:T(8,128)(2,1)S(1)}, u32[]{:S(2)}, u32[]{:S(2)}) %collective-permute-start.4) | collective-permute-done | bytes 1114144 | tf_op jit(solution)/shard_map/ppermute | solution.py:36
  133.1 4.3 %mix.2 = (bf16[16,544,128]{2,1,0:T(8,128)(2,1)S(1)}, bf16[16,272,128]{2,1,0:T(8,128)(2,1)S(1)}, f32[16,128,128]{2,1,0:T(8,128)S(1)}) custom-call(s32[18]{0:T(128)S(1)} %pad_add_fusion.index_ref, bf16[2,16,272,128]{3,2,1,0:T(8,128)(2,1)} %bitcast.34, bf16[16,272,128]{2,1,0:T(8,128)(2,1)S(1)} %collective-permute-done.4.refs_1_, ...), custom_call_target="tpu_custom_call" | custom-call | tf_op jit(solution)/shard_map/mix/pallas_call | solution.py:183
  137.4 1.4 copy-done.1
  138.8 1.0 copy-done.2
  140.8 7.7 %all-to-all-start.1 = ((bf16[16,544,128]{2,1,0:T(8,128)(2,1)}), bf16[16,544,128]{2,1,0:T(8,128)(2,1)S(1)}, u32[]{:S(2)}, u32[]{:S(2)}) async-start(bf16[16,544,128]{2,1,0:T(8,128)(2,1)} %copy-done.1), calls=%async_computation.3 | async-start | bytes 4456448 | tf_op jit(solution)/shard_map/all_to_all | solution.py:50
  148.4 16.7 %reduce-scatter.5.cloned.1.call-done = bf16[32,176,128]{2,1,0:T(8,128)(2,1)} async-done(((bf16[128,176,128]{2,1,0:T(8,128)(2,1)}), bf16[32,176,128]{2,1,0:T(8,128)(2,1)}) %reduce-scatter.5.cloned.1.call-update) | async-done | bytes 1441808 | tf_op jit(solution)/shard_map/reduce_scatter | solution.py:40
  165.2 2.0 dynamic-slice_bitcast_fusion.1
  167.2 2.7 %collective-permute-start.5 = (bf16[16,176,128]{2,1,0:T(8,128)(2,1)}, bf16[16,176,128]{2,1,0:T(8,128)(2,1)}, u32[]{:S(2)}, u32[]{:S(2)}) collective-permute-start(bf16[16,176,128]{2,1,0:T(8,128)(2,1)} %dynamic-slice_bitcast_fusion.1), channel_id=1, source_target_pairs={{0,16},{16,0},{32,48},{48,32},{64,80},{80,64},{96,112},{112,96},{1... | collective-permute-start | bytes 2162696 | tf_op jit(solution)/shard_map/ppermute | solution.py:36
  170.0 1.2 copy-done.7
  171.2 2.8 %add_pair.1.refs_0_ = bf16[4,16,64,128]{3,2,1,0:T(8,128)(2,1)S(1)} custom-call(s32[2]{0:T(128)S(1)} %pad_add_fusion.1.place_ref, bf16[4,2,16,512,128]{4,3,2,1,0:T(8,128)(2,1)} %bitcast.26, bf16[4,16,64,128]{3,2,1,0:T(8,128)(2,1)S(1)} %copy-done.7), custom_call_target="tpu_custom_call" | custom-call | tf_op jit(solution)/shard_map/add_pair/pallas_call | solution.py:100
  174.9 1.7 collective-permute-start.2
  176.6 1.6 collective-permute-start.3
  178.4 5.7 %renew.2.refs_0_ = bf16[2,16,512,128]{3,2,1,0:T(8,128)(2,1)} custom-call(s32[2]{0:T(128)S(1)} %fusion.filled_ref, bf16[2,16,512,128]{3,2,1,0:T(8,128)(2,1)} %bitcast.27, bf16[16,544,128]{2,1,0:T(8,128)(2,1)S(1)} %all-to-all-done.1.arrived_ref), custom_call_target="tpu_custom_call" | custom-call | tf_op jit(solution)/shard_map/renew/pallas_call | solution.py:278
  184.1 7.7 %collective-permute-done.5.refs_5_ = bf16[16,176,128]{2,1,0:T(8,128)(2,1)} collective-permute-done((bf16[16,176,128]{2,1,0:T(8,128)(2,1)}, bf16[16,176,128]{2,1,0:T(8,128)(2,1)}, u32[]{:S(2)}, u32[]{:S(2)}) %collective-permute-start.5) | collective-permute-done | bytes 720928 | tf_op jit(solution)/shard_map/ppermute | solution.py:36
  191.9 5.8 %mix.3 = (bf16[16,608,128]{2,1,0:T(8,128)(2,1)}, bf16[16,240,128]{2,1,0:T(8,128)(2,1)S(1)}) custom-call(s32[18]{0:T(128)S(1)} %pad_add_fusion.index_ref, bf16[4,16,64,128]{3,2,1,0:T(8,128)(2,1)S(1)} %add_pair.1.refs_0_, bf16[16,64,128]{2,1,0:T(8,128)(2,1)S(1)} %collective-permute-done.1.refs_1_, bf16[16,64,128]{2,1,0:T(8,128)(2,1)} %collective-permute-done.2.refs_2_, ...), custom_call_target="tpu_custom_call" | custom-call | tf_op jit(solution)/shard_map/mix/pallas_call | solution.py:183
  197.6 36.5 %all_to_all.21.parts_ref.arrived_ref = bf16[16,608,128]{2,1,0:T(8,128)(2,1)S(1)} all-to-all(bf16[16,608,128]{2,1,0:T(8,128)(2,1)} %get-tuple-element.38), channel_id=1, replica_groups=mesh['dp'=8,'mp'=16] {'mp'}, dimensions={0} | all-to-all | bytes 4980736 | tf_op jit(solution)/shard_map/all_to_all | solution.py:50
  234.1 2.1 polynomial.1
  236.2 4.4 %all-to-all-start.3 = ((bf16[16,128,128]{2,1,0:T(8,128)(2,1)}), bf16[16,128,128]{2,1,0:T(8,128)(2,1)S(1)}, u32[]{:S(2)}, u32[]{:S(2)}) async-start(bf16[16,128,128]{2,1,0:T(8,128)(2,1)} %polynomial.1), calls=%async_computation.5 | async-start | bytes 1048576 | tf_op jit(solution)/shard_map/all_to_all | solution.py:50
  240.6 4.6 %renew.3 = bf16[2,16,512,128]{3,2,1,0:T(8,128)(2,1)} custom-call(s32[2]{0:T(128)S(1)} %fusion.filled_ref, bf16[2,16,512,128]{3,2,1,0:T(8,128)(2,1)} %bitcast.28, bf16[16,608,128]{2,1,0:T(8,128)(2,1)S(1)} %all_to_all.21.parts_ref.arrived_ref, bf16[2,16,512,128]{3,2,1,0:T(8,128)(2,1)} %renew.2.refs_0_), custom_call_target="tpu_custom_call", output_to_operand_aliasing={{}: (3, {})} | custom-call | tf_op jit(solution)/shard_map/renew/pallas_call | solution.py:278
  245.2 5.4 %all-to-all-done.3.turn_ref = bf16[16,128,128]{2,1,0:T(8,128)(2,1)S(1)} async-done(((bf16[16,128,128]{2,1,0:T(8,128)(2,1)}), bf16[16,128,128]{2,1,0:T(8,128)(2,1)S(1)}, u32[]{:S(2)}, u32[]{:S(2)}) %all-to-all-start.3) | async-done | bytes 524320 | tf_op jit(solution)/shard_map/all_to_all | solution.py:50
  250.6 1.2 copy-done.3
  251.9 1.2 copy-done.9
  253.1 4.2 %turn_all.1 = bf16[16,512,128]{2,1,0:T(8,128)(2,1)} custom-call(bf16[16,240,128]{2,1,0:T(8,128)(2,1)S(1)} %copy-done.9, bf16[16,272,128]{2,1,0:T(8,128)(2,1)S(1)} %copy-done.3, bf16[16,128,128]{2,1,0:T(8,128)(2,1)S(1)} %all-to-all-done.3.turn_ref), custom_call_target="tpu_custom_call" | custom-call | tf_op jit(solution)/shard_map/turn_all/pallas_call | solution.py:248
  (36 shorter events, 3.1 us)
Async XLA Ops:
  7.2 99.0 %reduce-scatter.3.cloned.1.call-start = ((), (), s32[]{:S(2)}) async-start(), calls=%async_computation.6 | async-start | bytes 11141120 | tf_op jit(solution)/shard_map/reduce_scatter | solution.py:40
  14.9 150.3 %reduce-scatter.5.cloned.1.call-start = ((), (), s32[]{:S(2)}) async-start(), calls=%async_computation.7 | async-start | bytes 7208960 | tf_op jit(solution)/shard_map/reduce_scatter | solution.py:40
  15.0 2.9 %copy-start.10 = (bf16[1,1,2,8192,128]{4,3,2,1,0:T(8,128)(2,1)S(1)}, bf16[1,1,2,8192,128]{4,3,2,1,0:T(8,128)(2,1)}, u32[]{:S(2)}) copy-start(bf16[1,1,2,8192,128]{4,3,2,1,0:T(8,128)(2,1)} %param.4) | copy-start | bytes 12582916
  80.0 30.1 %copy-start.11 = (s32[1,16,2]{1,2,0:T(2,128)S(1)}, s32[1,16,2]{1,2,0:T(2,128)}, u32[]{:S(2)}) copy-start(s32[1,16,2]{1,2,0:T(2,128)} %param.5) | copy-start | bytes 388
  80.0 25.1 %collective-permute-start = (bf16[4,16,64,128]{3,2,1,0:T(8,128)(2,1)S(1)}, bf16[4,16,64,128]{3,2,1,0:T(8,128)(2,1)S(1)}, u32[]{:S(2)}, u32[]{:S(2)}) collective-permute-start(bf16[4,16,64,128]{3,2,1,0:T(8,128)(2,1)S(1)} %copy_rows.1), channel_id=1, source_target_pairs={{0,16},{16,0},{32,48},{48,32},{64,80},{80,64},{96,112},{112,96},{1... | collective-permute-start | bytes 3145736 | tf_op jit(solution)/shard_map/ppermute | solution.py:36
  105.2 1.0 copy-start.6
  107.5 25.6 %collective-permute-start.4 = (bf16[16,272,128]{2,1,0:T(8,128)(2,1)S(1)}, bf16[16,272,128]{2,1,0:T(8,128)(2,1)S(1)}, u32[]{:S(2)}, u32[]{:S(2)}) collective-permute-start(bf16[16,272,128]{2,1,0:T(8,128)(2,1)S(1)} %dynamic-slice_bitcast_fusion), channel_id=1, source_target_pairs={{0,16},{16,0},{32,48},{48,32},{64,80},{80,64},{96,112},{112,96},{1... | collective-permute-start | bytes 3342344 | tf_op jit(solution)/shard_map/ppermute | solution.py:36
  137.4 1.4 copy-start.1
  138.8 1.0 copy-start.2
  139.8 1.0 copy-start.4
  140.8 37.6 %all-to-all-start.1 = ((bf16[16,544,128]{2,1,0:T(8,128)(2,1)}), bf16[16,544,128]{2,1,0:T(8,128)(2,1)S(1)}, u32[]{:S(2)}, u32[]{:S(2)}) async-start(bf16[16,544,128]{2,1,0:T(8,128)(2,1)} %copy-done.1), calls=%async_computation.3 | async-start | bytes 4456448 | tf_op jit(solution)/shard_map/all_to_all | solution.py:50
  167.2 24.6 %collective-permute-start.5 = (bf16[16,176,128]{2,1,0:T(8,128)(2,1)}, bf16[16,176,128]{2,1,0:T(8,128)(2,1)}, u32[]{:S(2)}, u32[]{:S(2)}) collective-permute-start(bf16[16,176,128]{2,1,0:T(8,128)(2,1)} %dynamic-slice_bitcast_fusion.1), channel_id=1, source_target_pairs={{0,16},{16,0},{32,48},{48,32},{64,80},{80,64},{96,112},{112,96},{1... | collective-permute-start | bytes 2162696 | tf_op jit(solution)/shard_map/ppermute | solution.py:36
  170.0 1.2 copy-start.7
  174.9 16.9 %collective-permute-start.1 = (bf16[16,64,128]{2,1,0:T(8,128)(2,1)}, bf16[16,64,128]{2,1,0:T(8,128)(2,1)S(1)}, u32[]{:S(2)}, u32[]{:S(2)}) collective-permute-start(bf16[16,64,128]{2,1,0:T(8,128)(2,1)} %get-tuple-element.42), channel_id=1, source_target_pairs={{0,32},{16,48},{32,64},{48,80},{64,96},{80,112},{96,0},{112,16},{1... | collective-permute-start | bytes 786440 | tf_op jit(solution)/shard_map/ppermute | solution.py:57
  174.9 16.9 %collective-permute-start.2 = (bf16[16,64,128]{2,1,0:T(8,128)(2,1)}, bf16[16,64,128]{2,1,0:T(8,128)(2,1)}, u32[]{:S(2)}, u32[]{:S(2)}) collective-permute-start(bf16[16,64,128]{2,1,0:T(8,128)(2,1)} %get-tuple-element.41), channel_id=1, source_target_pairs={{0,64},{16,80},{32,96},{48,112},{64,0},{80,16},{96,32},{112,48},{1... | collective-permute-start | bytes 786440 | tf_op jit(solution)/shard_map/ppermute | solution.py:57
  176.6 15.3 %collective-permute-start.3 = (bf16[16,64,128]{2,1,0:T(8,128)(2,1)}, bf16[16,64,128]{2,1,0:T(8,128)(2,1)}, u32[]{:S(2)}, u32[]{:S(2)}) collective-permute-start(bf16[16,64,128]{2,1,0:T(8,128)(2,1)} %get-tuple-element.40), channel_id=1, source_target_pairs={{0,96},{16,112},{32,0},{48,16},{64,32},{80,48},{96,64},{112,80},{1... | collective-permute-start | bytes 786440 | tf_op jit(solution)/shard_map/ppermute | solution.py:57
  178.4 13.5 %copy-start = (bf16[32,176,128]{2,1,0:T(8,128)(2,1)S(1)}, bf16[32,176,128]{2,1,0:T(8,128)(2,1)}, u32[]{:S(2)}) copy-start(bf16[32,176,128]{2,1,0:T(8,128)(2,1)} %reduce-scatter.5.cloned.1.call-done) | copy-start | bytes 4325380
  178.4 13.5 %copy-start.5 = (f32[16,128,128]{2,1,0:T(8,128)S(1)}, f32[16,128,128]{2,1,0:T(8,128)}, u32[]{:S(2)}) copy-start(f32[16,128,128]{2,1,0:T(8,128)} %copy-done.4) | copy-start | bytes 3145732
  197.6 36.5 %copy-start.8 = (bf16[16,240,128]{2,1,0:T(8,128)(2,1)}, bf16[16,240,128]{2,1,0:T(8,128)(2,1)S(1)}, u32[]{:S(2)}) copy-start(bf16[16,240,128]{2,1,0:T(8,128)(2,1)S(1)} %get-tuple-element.36.last_ref) | copy-start | bytes 2949124
  236.2 14.4 %all-to-all-start.3 = ((bf16[16,128,128]{2,1,0:T(8,128)(2,1)}), bf16[16,128,128]{2,1,0:T(8,128)(2,1)S(1)}, u32[]{:S(2)}, u32[]{:S(2)}) async-start(bf16[16,128,128]{2,1,0:T(8,128)(2,1)} %polynomial.1), calls=%async_computation.5 | async-start | bytes 1048576 | tf_op jit(solution)/shard_map/all_to_all | solution.py:50
  250.6 1.2 copy-start.3
  251.9 1.2 copy-start.9
Sparse Core Ops, SparseCore 0:
  15.0 88.2 reduce-scatter.2
  105.7 59.4 reduce-scatter.4

commit v4 on v3

--- a/solution.py
+++ b/solution.py
@@ -22,10 +22,11 @@
 PAIRED, LATE, EARLY = (0, 64), (64, 176), (240, 272)
 LAST = (0, 240)
 VMEM = 48 * 1024 * 1024
-
-
-def params():
-    return pltpu.CompilerParams(vmem_limit_bytes=VMEM)
+MOST_VMEM = 60 * 1024 * 1024
+
+
+def params(limit=VMEM):
+    return pltpu.CompilerParams(vmem_limit_bytes=limit)
 
 
 def z_groups():
@@ -189,7 +190,7 @@
             out_specs=[whole(*shape.shape) for shape in shapes],
         ),
         out_shape=shapes,
-        compiler_params=params(),
+        compiler_params=params(VMEM if last else MOST_VMEM),
         name="mix",
     )(index, *operands)
 

time: 265 us -> 263 us (level)
  local copies, waits for them, and re-layouts: 26.2 us -> 22.3 us
    unnamed x25 -> x21, local copies, waits for them, and re-layouts: 8.08 us -> 3.78 us
  transfers between devices with their start and end apart: 10 -> 10, of which waited for: 5 -> 5; matrix products, arithmetic and copies ran while one was open for 4% -> 5% of each run, Pallas kernels for 8% -> 9%
where the time goes in v4:
time: 263 us
  blocking collectives  92.7 us (35%)
  waiting for transfers between devices  74.2 us (28%)
  Pallas kernels  34.7 us (13%)
  starting transfers between devices  23.5 us (9%)
  local copies, waits for them, and re-layouts  22.3 us (8%)
  between operations  14.2 us (5%)
    all_to_all x2, blocking collectives, exchange(): return lax.all_to_all(x, 'mp', split_axis=0, concat_axis=0, tiled=True)  92.7 us
    ppermute x3, waiting for transfers between devices, swap_y(): return lax.ppermute(x, 'dp', [(i, i ^ 1) for i in range(Z_SIZE * Y_SIZE)])  50.4 us
    reduce_scatter x2, waiting for transfers between devices, scatter_z(): lax.psum_scatter(x, 'dp', scatter_dimension=0, tiled=True, axis_index_gro...  18.3 us
    pallas_call x2, Pallas kernels, mix(): pl.pallas_call(body, grid_spec=pltpu.PrefetchScalarGridSpec(num_scalar_pr...  12.4 us
    all_to_all x2, starting transfers between devices, exchange(): return lax.all_to_all(x, 'mp', split_axis=0, concat_axis=0, tiled=True)  12 us
    pallas_call x2, Pallas kernels, renew(): pl.pallas_call(body, grid_spec=pltpu.PrefetchScalarGridSpec(num_scalar_pr...  10.3 us
    ppermute x3, starting transfers between devices, swap_y(): return lax.ppermute(x, 'dp', [(i, i ^ 1) for i in range(Z_SIZE * Y_SIZE)])  8.11 us
    slice x1, local copies, waits for them, and re-layouts, on_device(): early, own1 = barrier(own[:, :, :, EARLY[0]:EARLY[0] + EARLY[1]], own)  7.64 us
  transfers between devices with their start and end apart: 10, of which 5 were waited for; matrix products, arithmetic and copies ran while one was open for 5% of the time, Pallas kernels for 9%

profile of v4, /device:TPU:1, one launch (start us, length us, event | category | flops | bytes accessed | tf_op | source)
XLA Modules:
  0.0 262.6 jit_solution(13568194786263401856)
XLA Ops:
  7.2 7.6 %slice.8 = bf16[4,2,16,272,128]{4,3,2,1,0:T(8,128)(2,1)} slice(bf16[4,2,16,512,128]{4,3,2,1,0:T(8,128)(2,1)} %bitcast.23), slice={[0:4], [0:2], [0:16], [240:512], [0:128]} | slice | bytes 17825792 | tf_op jit(solution)/shard_map/slice | solution.py:326
  15.0 2.9 %copy_rows.1 = bf16[4,16,64,128]{3,2,1,0:T(8,128)(2,1)S(1)} custom-call(s32[2]{0:T(128)S(1)} %pad_add_fusion.1.place_ref, bf16[4,2,16,512,128]{4,3,2,1,0:T(8,128)(2,1)} %bitcast.24), custom_call_target="tpu_custom_call" | custom-call | tf_op jit(solution)/shard_map/copy_rows/pallas_call | solution.py:73
  17.9 0.4 copy.15
  18.4 55.9 %all_to_all.20.refs_2_.refs_6_ = bf16[16,2,512,128]{3,2,1,0:T(8,128)(2,1)} all-to-all(bf16[16,2,512,128]{3,2,1,0:T(8,128)(2,1)S(1)} %copy.15), channel_id=1, replica_groups=mesh['dp'=8,'mp'=16] {'mp'}, dimensions={0} | all-to-all | bytes 8388608 | tf_op jit(solution)/shard_map/all_to_all | solution.py:51
  74.3 5.7 %slice.7 = bf16[4,2,16,176,128]{4,3,2,1,0:T(8,128)(2,1)} slice(bf16[4,2,16,512,128]{4,3,2,1,0:T(8,128)(2,1)} %bitcast.25), slice={[0:4], [0:2], [0:16], [64:240], [0:128]} | slice | bytes 11534336 | tf_op jit(solution)/shard_map/slice | solution.py:333
  80.0 2.7 %collective-permute-start = (bf16[4,16,64,128]{3,2,1,0:T(8,128)(2,1)S(1)}, bf16[4,16,64,128]{3,2,1,0:T(8,128)(2,1)S(1)}, u32[]{:S(2)}, u32[]{:S(2)}) collective-permute-start(bf16[4,16,64,128]{3,2,1,0:T(8,128)(2,1)S(1)} %copy_rows.1), channel_id=1, source_target_pairs={{0,16},{16,0},{32,48},{48,32},{64,80},{80,64},{96,112},{112,96},{1... | collective-permute-start | bytes 3145736 | tf_op jit(solution)/shard_map/ppermute | solution.py:37
  82.7 22.5 %collective-permute-done.received_ref = bf16[4,16,64,128]{3,2,1,0:T(8,128)(2,1)S(1)} collective-permute-done((bf16[4,16,64,128]{3,2,1,0:T(8,128)(2,1)S(1)}, bf16[4,16,64,128]{3,2,1,0:T(8,128)(2,1)S(1)}, u32[]{:S(2)}, u32[]{:S(2)}) %collective-permute-start) | collective-permute-done | bytes 1048608 | tf_op jit(solution)/shard_map/ppermute | solution.py:37
  105.2 1.7 dynamic-slice_bitcast_fusion
  106.9 2.7 %collective-permute-start.4 = (bf16[16,272,128]{2,1,0:T(8,128)(2,1)S(1)}, bf16[16,272,128]{2,1,0:T(8,128)(2,1)}, u32[]{:S(2)}, u32[]{:S(2)}) collective-permute-start(bf16[16,272,128]{2,1,0:T(8,128)(2,1)S(1)} %dynamic-slice_bitcast_fusion), channel_id=1, source_target_pairs={{0,16},{16,0},{32,48},{48,32},{64,80},{80,64},{96,112},{112,96},{1... | collective-permute-start | bytes 3342344 | tf_op jit(solution)/shard_map/ppermute | solution.py:37
  109.9 0.7 pad_add_fusion.index_ref
  110.5 22.1 %collective-permute-done.4.refs_1_ = bf16[16,272,128]{2,1,0:T(8,128)(2,1)} collective-permute-done((bf16[16,272,128]{2,1,0:T(8,128)(2,1)S(1)}, bf16[16,272,128]{2,1,0:T(8,128)(2,1)}, u32[]{:S(2)}, u32[]{:S(2)}) %collective-permute-start.4) | collective-permute-done | bytes 1114144 | tf_op jit(solution)/shard_map/ppermute | solution.py:37
  132.6 6.7 %mix.2 = (bf16[16,544,128]{2,1,0:T(8,128)(2,1)}, bf16[16,272,128]{2,1,0:T(8,128)(2,1)}, f32[16,128,128]{2,1,0:T(8,128)}) custom-call(s32[18]{0:T(128)} %pad_add_fusion.index_ref, bf16[2,16,272,128]{3,2,1,0:T(8,128)(2,1)} %bitcast.34, bf16[16,272,128]{2,1,0:T(8,128)(2,1)} %collective-permute-done.4.refs_1_, bf16[16,2,512,128]{3,2,1,0:T(8,128)(2,1)} %all_to_all.20.refs_2_.refs_6_), custom_call_target="tpu_custom_call" | custom-call | tf_op jit(solution)/shard_map/mix/pallas_call | solution.py:184
  139.3 7.6 %all-to-all-start.1 = ((bf16[16,544,128]{2,1,0:T(8,128)(2,1)}), bf16[16,544,128]{2,1,0:T(8,128)(2,1)S(1)}, u32[]{:S(2)}, u32[]{:S(2)}) async-start(bf16[16,544,128]{2,1,0:T(8,128)(2,1)} %get-tuple-element.32), calls=%async_computation.3 | async-start | bytes 4456448 | tf_op jit(solution)/shard_map/all_to_all | solution.py:51
  146.9 18.3 %reduce-scatter.5.cloned.1.call-done = bf16[32,176,128]{2,1,0:T(8,128)(2,1)} async-done(((bf16[128,176,128]{2,1,0:T(8,128)(2,1)}), bf16[32,176,128]{2,1,0:T(8,128)(2,1)}) %reduce-scatter.5.cloned.1.call-update) | async-done | bytes 1441808 | tf_op jit(solution)/shard_map/reduce_scatter | solution.py:41
  165.2 2.0 dynamic-slice_bitcast_fusion.1
  167.2 2.7 %collective-permute-start.5 = (bf16[16,176,128]{2,1,0:T(8,128)(2,1)}, bf16[16,176,128]{2,1,0:T(8,128)(2,1)}, u32[]{:S(2)}, u32[]{:S(2)}) collective-permute-start(bf16[16,176,128]{2,1,0:T(8,128)(2,1)} %dynamic-slice_bitcast_fusion.1), channel_id=1, source_target_pairs={{0,16},{16,0},{32,48},{48,32},{64,80},{80,64},{96,112},{112,96},{1... | collective-permute-start | bytes 2162696 | tf_op jit(solution)/shard_map/ppermute | solution.py:37
  170.0 1.2 copy-done.4
  171.2 2.8 %add_pair.1.refs_0_ = bf16[4,16,64,128]{3,2,1,0:T(8,128)(2,1)S(1)} custom-call(s32[2]{0:T(128)S(1)} %pad_add_fusion.1.place_ref, bf16[4,2,16,512,128]{4,3,2,1,0:T(8,128)(2,1)} %bitcast.26, bf16[4,16,64,128]{3,2,1,0:T(8,128)(2,1)S(1)} %copy-done.4), custom_call_target="tpu_custom_call" | custom-call | tf_op jit(solution)/shard_map/add_pair/pallas_call | solution.py:101
  174.0 0.9 dynamic-slice_bitcast_fusion.2
  174.9 1.7 collective-permute-start.2
  176.5 1.6 collective-permute-start.3
  178.4 5.7 %renew.2.refs_0_ = bf16[2,16,512,128]{3,2,1,0:T(8,128)(2,1)} custom-call(s32[2]{0:T(128)S(1)} %fusion.filled_ref, bf16[2,16,512,128]{3,2,1,0:T(8,128)(2,1)} %bitcast.27, bf16[16,544,128]{2,1,0:T(8,128)(2,1)S(1)} %all-to-all-done.1.arrived_ref), custom_call_target="tpu_custom_call" | custom-call | tf_op jit(solution)/shard_map/renew/pallas_call | solution.py:279
  184.1 5.9 %collective-permute-done.5.refs_5_ = bf16[16,176,128]{2,1,0:T(8,128)(2,1)} collective-permute-done((bf16[16,176,128]{2,1,0:T(8,128)(2,1)}, bf16[16,176,128]{2,1,0:T(8,128)(2,1)}, u32[]{:S(2)}, u32[]{:S(2)}) %collective-permute-start.5) | collective-permute-done | bytes 720928 | tf_op jit(solution)/shard_map/ppermute | solution.py:37
  190.0 5.8 %mix.3 = (bf16[16,608,128]{2,1,0:T(8,128)(2,1)}, bf16[16,240,128]{2,1,0:T(8,128)(2,1)S(1)}) custom-call(s32[18]{0:T(128)S(1)} %copy-done.7, bf16[4,16,64,128]{3,2,1,0:T(8,128)(2,1)S(1)} %add_pair.1.refs_0_, bf16[16,64,128]{2,1,0:T(8,128)(2,1)S(1)} %collective-permute-done.1.refs_1_, bf16[16,64,128]{2,1,0:T(8,128)(2,1)} %collective-permute-done.2.refs_2_, ...), custom_call_target="tpu_custom_call" | custom-call | tf_op jit(solution)/shard_map/mix/pallas_call | solution.py:184
  195.8 36.8 %all_to_all.21.parts_ref.arrived_ref = bf16[16,608,128]{2,1,0:T(8,128)(2,1)S(1)} all-to-all(bf16[16,608,128]{2,1,0:T(8,128)(2,1)} %get-tuple-element.38), channel_id=1, replica_groups=mesh['dp'=8,'mp'=16] {'mp'}, dimensions={0} | all-to-all | bytes 4980736 | tf_op jit(solution)/shard_map/all_to_all | solution.py:51
  232.6 2.1 polynomial.1
  234.7 4.4 %all-to-all-start.3 = ((bf16[16,128,128]{2,1,0:T(8,128)(2,1)}), bf16[16,128,128]{2,1,0:T(8,128)(2,1)S(1)}, u32[]{:S(2)}, u32[]{:S(2)}) async-start(bf16[16,128,128]{2,1,0:T(8,128)(2,1)} %polynomial.1), calls=%async_computation.5 | async-start | bytes 1048576 | tf_op jit(solution)/shard_map/all_to_all | solution.py:51
  239.1 4.6 %renew.3 = bf16[2,16,512,128]{3,2,1,0:T(8,128)(2,1)} custom-call(s32[2]{0:T(128)S(1)} %fusion.filled_ref, bf16[2,16,512,128]{3,2,1,0:T(8,128)(2,1)} %bitcast.28, bf16[16,608,128]{2,1,0:T(8,128)(2,1)S(1)} %all_to_all.21.parts_ref.arrived_ref, bf16[2,16,512,128]{3,2,1,0:T(8,128)(2,1)} %renew.2.refs_0_), custom_call_target="tpu_custom_call", output_to_operand_aliasing={{}: (3, {})} | custom-call | tf_op jit(solution)/shard_map/renew/pallas_call | solution.py:279
  243.7 5.4 %all-to-all-done.3.turn_ref = bf16[16,128,128]{2,1,0:T(8,128)(2,1)S(1)} async-done(((bf16[16,128,128]{2,1,0:T(8,128)(2,1)}), bf16[16,128,128]{2,1,0:T(8,128)(2,1)S(1)}, u32[]{:S(2)}, u32[]{:S(2)}) %all-to-all-start.3) | async-done | bytes 524320 | tf_op jit(solution)/shard_map/all_to_all | solution.py:51
  249.1 1.2 copy-done.1
  250.3 1.2 copy-done.6
  251.5 4.2 %turn_all.1 = bf16[16,512,128]{2,1,0:T(8,128)(2,1)} custom-call(bf16[16,240,128]{2,1,0:T(8,128)(2,1)S(1)} %copy-done.6, bf16[16,272,128]{2,1,0:T(8,128)(2,1)S(1)} %copy-done.1, bf16[16,128,128]{2,1,0:T(8,128)(2,1)S(1)} %all-to-all-done.3.turn_ref), custom_call_target="tpu_custom_call" | custom-call | tf_op jit(solution)/shard_map/turn_all/pallas_call | solution.py:249
  (32 shorter events, 0.7 us)
Async XLA Ops:
  7.2 98.0 %reduce-scatter.3.cloned.1.call-start = ((), (), s32[]{:S(2)}) async-start(), calls=%async_computation.6 | async-start | bytes 11141120 | tf_op jit(solution)/shard_map/reduce_scatter | solution.py:41
  14.9 150.3 %reduce-scatter.5.cloned.1.call-start = ((), (), s32[]{:S(2)}) async-start(), calls=%async_computation.7 | async-start | bytes 7208960 | tf_op jit(solution)/shard_map/reduce_scatter | solution.py:41
  15.0 2.9 %copy-start.8 = (bf16[1,1,2,8192,128]{4,3,2,1,0:T(8,128)(2,1)S(1)}, bf16[1,1,2,8192,128]{4,3,2,1,0:T(8,128)(2,1)}, u32[]{:S(2)}) copy-start(bf16[1,1,2,8192,128]{4,3,2,1,0:T(8,128)(2,1)} %param.4) | copy-start | bytes 12582916
  80.0 29.5 %copy-start.9 = (s32[1,16,2]{1,2,0:T(2,128)S(1)}, s32[1,16,2]{1,2,0:T(2,128)}, u32[]{:S(2)}) copy-start(s32[1,16,2]{1,2,0:T(2,128)} %param.5) | copy-start | bytes 388
  80.0 25.1 %collective-permute-start = (bf16[4,16,64,128]{3,2,1,0:T(8,128)(2,1)S(1)}, bf16[4,16,64,128]{3,2,1,0:T(8,128)(2,1)S(1)}, u32[]{:S(2)}, u32[]{:S(2)}) collective-permute-start(bf16[4,16,64,128]{3,2,1,0:T(8,128)(2,1)S(1)} %copy_rows.1), channel_id=1, source_target_pairs={{0,16},{16,0},{32,48},{48,32},{64,80},{80,64},{96,112},{112,96},{1... | collective-permute-start | bytes 3145736 | tf_op jit(solution)/shard_map/ppermute | solution.py:37
  105.2 34.1 %copy-start.3 = (bf16[4,16,64,128]{3,2,1,0:T(8,128)(2,1)}, bf16[4,16,64,128]{3,2,1,0:T(8,128)(2,1)S(1)}, u32[]{:S(2)}) copy-start(bf16[4,16,64,128]{3,2,1,0:T(8,128)(2,1)S(1)} %collective-permute-done.received_ref) | copy-start | bytes 3145732
  106.9 25.7 %collective-permute-start.4 = (bf16[16,272,128]{2,1,0:T(8,128)(2,1)S(1)}, bf16[16,272,128]{2,1,0:T(8,128)(2,1)}, u32[]{:S(2)}, u32[]{:S(2)}) collective-permute-start(bf16[16,272,128]{2,1,0:T(8,128)(2,1)S(1)} %dynamic-slice_bitcast_fusion), channel_id=1, source_target_pairs={{0,16},{16,0},{32,48},{48,32},{64,80},{80,64},{96,112},{112,96},{1... | collective-permute-start | bytes 3342344 | tf_op jit(solution)/shard_map/ppermute | solution.py:37
  139.3 39.1 %all-to-all-start.1 = ((bf16[16,544,128]{2,1,0:T(8,128)(2,1)}), bf16[16,544,128]{2,1,0:T(8,128)(2,1)S(1)}, u32[]{:S(2)}, u32[]{:S(2)}) async-start(bf16[16,544,128]{2,1,0:T(8,128)(2,1)} %get-tuple-element.32), calls=%async_computation.3 | async-start | bytes 4456448 | tf_op jit(solution)/shard_map/all_to_all | solution.py:51
  167.2 22.7 %collective-permute-start.5 = (bf16[16,176,128]{2,1,0:T(8,128)(2,1)}, bf16[16,176,128]{2,1,0:T(8,128)(2,1)}, u32[]{:S(2)}, u32[]{:S(2)}) collective-permute-start(bf16[16,176,128]{2,1,0:T(8,128)(2,1)} %dynamic-slice_bitcast_fusion.1), channel_id=1, source_target_pairs={{0,16},{16,0},{32,48},{48,32},{64,80},{80,64},{96,112},{112,96},{1... | collective-permute-start | bytes 2162696 | tf_op jit(solution)/shard_map/ppermute | solution.py:37
  170.0 1.2 copy-start.4
  174.9 15.1 %collective-permute-start.1 = (bf16[16,64,128]{2,1,0:T(8,128)(2,1)}, bf16[16,64,128]{2,1,0:T(8,128)(2,1)S(1)}, u32[]{:S(2)}, u32[]{:S(2)}) collective-permute-start(bf16[16,64,128]{2,1,0:T(8,128)(2,1)} %get-tuple-element.42), channel_id=1, source_target_pairs={{0,32},{16,48},{32,64},{48,80},{64,96},{80,112},{96,0},{112,16},{1... | collective-permute-start | bytes 786440 | tf_op jit(solution)/shard_map/ppermute | solution.py:58
  174.9 15.1 %collective-permute-start.2 = (bf16[16,64,128]{2,1,0:T(8,128)(2,1)}, bf16[16,64,128]{2,1,0:T(8,128)(2,1)}, u32[]{:S(2)}, u32[]{:S(2)}) collective-permute-start(bf16[16,64,128]{2,1,0:T(8,128)(2,1)} %get-tuple-element.41), channel_id=1, source_target_pairs={{0,64},{16,80},{32,96},{48,112},{64,0},{80,16},{96,32},{112,48},{1... | collective-permute-start | bytes 786440 | tf_op jit(solution)/shard_map/ppermute | solution.py:58
  176.5 13.4 %collective-permute-start.3 = (bf16[16,64,128]{2,1,0:T(8,128)(2,1)}, bf16[16,64,128]{2,1,0:T(8,128)(2,1)}, u32[]{:S(2)}, u32[]{:S(2)}) collective-permute-start(bf16[16,64,128]{2,1,0:T(8,128)(2,1)} %get-tuple-element.40), channel_id=1, source_target_pairs={{0,96},{16,112},{32,0},{48,16},{64,32},{80,48},{96,64},{112,80},{1... | collective-permute-start | bytes 786440 | tf_op jit(solution)/shard_map/ppermute | solution.py:58
  178.3 11.6 %copy-start = (bf16[32,176,128]{2,1,0:T(8,128)(2,1)S(1)}, bf16[32,176,128]{2,1,0:T(8,128)(2,1)}, u32[]{:S(2)}) copy-start(bf16[32,176,128]{2,1,0:T(8,128)(2,1)} %reduce-scatter.5.cloned.1.call-done) | copy-start | bytes 4325380
  178.3 11.6 %copy-start.2 = (f32[16,128,128]{2,1,0:T(8,128)S(1)}, f32[16,128,128]{2,1,0:T(8,128)}, u32[]{:S(2)}) copy-start(f32[16,128,128]{2,1,0:T(8,128)} %get-tuple-element.35.refs_7_) | copy-start | bytes 3145732
  178.4 11.6 %copy-start.7 = (s32[18]{0:T(128)S(1)}, s32[18]{0:T(128)}, u32[]{:S(2)}) copy-start(s32[18]{0:T(128)} %pad_add_fusion.index_ref) | copy-start | bytes 220
  195.8 36.8 %copy-start.5 = (bf16[16,240,128]{2,1,0:T(8,128)(2,1)}, bf16[16,240,128]{2,1,0:T(8,128)(2,1)S(1)}, u32[]{:S(2)}) copy-start(bf16[16,240,128]{2,1,0:T(8,128)(2,1)S(1)} %get-tuple-element.36.last_ref) | copy-start | bytes 2949124
  234.7 14.4 %all-to-all-start.3 = ((bf16[16,128,128]{2,1,0:T(8,128)(2,1)}), bf16[16,128,128]{2,1,0:T(8,128)(2,1)S(1)}, u32[]{:S(2)}, u32[]{:S(2)}) async-start(bf16[16,128,128]{2,1,0:T(8,128)(2,1)} %polynomial.1), calls=%async_computation.5 | async-start | bytes 1048576 | tf_op jit(solution)/shard_map/all_to_all | solution.py:51
  249.1 1.2 copy-start.1
  250.3 1.2 copy-start.6
Sparse Core Ops, SparseCore 0:
  15.0 88.2 reduce-scatter.2
  105.7 59.4 reduce-scatter.4
